TPU v7x, 32 devices: a whole 2x2x4 slice. The times are simulated.
32 devices in a mesh: dp: 8 (over z, x), expert: 4 (over y, core).
Axes of the slice: x: 2, y: 2, z: 4, core: 2. Of those that a mesh axis runs over, the one named last changes fastest.
Arguments:
- out_grad: bfloat16 [512, 3072], P('expert'), may hold values from -1.1953125 to 1.1953125
- routes: int32 [512, 4], P('expert'), may hold values from 0 to 7, all different within a row; in each aligned block of 128 rows (0 to 127, 128 to 255, ...) at most 80 rows name the same one
- gate_values: float32 [512, 4], P('expert'), may hold values from 0.1 to 0.5
- layer_input: bfloat16 [512, 3072], P('expert'), may hold values from -6 to 6
- w_gate: bfloat16 [8, 3072, 8192], P('expert', None, 'dp'), may hold values from -0.109375 to 0.109375
- w_up: bfloat16 [8, 3072, 8192], P('expert', None, 'dp'), may hold values from -0.109375 to 0.109375
- w_down: bfloat16 [8, 3072, 8192], P('expert', None, 'dp'), may hold values from -0.109375 to 0.109375
Outputs:
- input_grad: bfloat16 [512, 3072], P('expert')
- grad_gate: float32 [8, 3072, 8192], P('expert', None, 'dp')
- grad_up: float32 [8, 3072, 8192], P('expert', None, 'dp')
Inputs may be any that keep to these rules, and one draw needn't show every extreme that they name: In every aligned block of 128 tokens (the tokens of one index of expert) no expert is named by more than 80 routes, a bound that some block reaches; the 4 experts of a token differ.
All inputs are finite; a program needn't handle non-finite values.
Results may differ from a plain program's by a relative error of at most 0.024.
Values may be sent and summed in bfloat16 or wider, within the bound.
No kernel may reach another device: no remote copies, remote signals or barrier semaphores. Data moves between devices by JAX's collectives and lax.ppermute only.
A program may use at most 192 MiB of HBM per device.

v0:
```python
import functools

import jax
import jax.numpy as jnp
from jax import lax
from jax.experimental import pallas as pl
from jax.experimental.pallas import tpu as pltpu
from jax.sharding import PartitionSpec as P

EXPERTS = 8
MOST = 80
UNIT_TILE = 512
FEATURE_TILE = 512
BF16 = jnp.bfloat16
F32 = jnp.float32
NN = (((1,), (0,)), ((), ()))
NT = (((1,), (1,)), ((), ()))
TN = (((0,), (0,)), ((), ()))


def dot(a, b, dims=NN):
    return lax.dot_general(a, b, dims, preferred_element_type=F32)


def params(count, mebibytes):
    return pltpu.CompilerParams(
        dimension_semantics=("arbitrary",) * count, vmem_limit_bytes=mebibytes * 1024 * 1024
    )


def whole(shape):
    return pl.BlockSpec(
        shape, lambda *_: (0,) * len(shape), pipeline_mode=pl.Buffered(buffer_count=1)
    )


def one_hot(slot_row):
    slots = lax.broadcasted_iota(jnp.int32, (MOST, slot_row.shape[1]), 0)
    return slots == slot_row.astype(jnp.int32)


def lay_out(held, pieces, first):
    rows, at = held.shape[0], 0
    for piece in pieces:
        low, high = max(first, at), min(first + rows, at + piece.shape[0])
        if low < high:
            held[low - first : high - first] = piece[low - at : high - at]
        at += piece.shape[0]


def column_chunks(features):
    step = 768 if features % 768 == 0 else features
    return [slice(c, c + step) for c in range(0, features, step)]


def dispatch(pieces, slot, held, chosen, out, weight=None):
    experts, blocks, tokens = slot.shape
    group = held.shape[0] // tokens
    places = [(l, b) for l in range(experts) for b in range(group)]
    for start in range(0, blocks, group):
        chosen[...] = jnp.zeros_like(chosen)
        scales = []
        for i, (l, b) in enumerate(places):
            at = slice(start + b, start + b + 1)
            mask = one_hot(slot[l, at, :])
            chosen[i * MOST : (i + 1) * MOST, b * tokens : (b + 1) * tokens] = mask.astype(BF16)
            if weight is not None:
                scales.append(
                    jnp.sum(jnp.where(mask, weight[l, at, :], 0.0), axis=1, keepdims=True)
                )
        lay_out(held, pieces, start * tokens)
        for cols in column_chunks(held.shape[1]):
            taken = dot(chosen[...], held[:, cols])
            for i, (l, b) in enumerate(places):
                part = taken[i * MOST : (i + 1) * MOST]
                if scales:
                    part = part * scales[i]
                span = slice((start + b) * MOST, (start + b + 1) * MOST)
                out[l, span, cols] = part.astype(BF16)


def dispatch_scratch(experts, blocks, tokens, features):
    group = 2 if blocks % 2 == 0 else 1
    return [
        pltpu.VMEM((group * tokens, features), BF16),
        pltpu.VMEM((experts * group * MOST, group * tokens), BF16),
        pltpu.VMEM((experts, blocks * MOST, features), BF16),
    ]


def weight_tiles(step, matrices, buffers, ready):
    _, features, tile = buffers[0].shape
    tiles = matrices[0].shape[2] // tile
    cols = pl.ds(pl.multiple_of(step % tiles * tile, tile), tile)
    return [
        pltpu.make_async_copy(
            matrix.at[step // tiles, :, cols], buffer.at[step % 2], ready.at[step % 2, i]
        )
        for i, (matrix, buffer) in enumerate(zip(matrices, buffers))
    ]


def next_tiles(step, matrices, buffers, ready):
    @pl.when(step + 1 < pl.num_programs(0))
    def _():
        for copy in weight_tiles(step + 1, matrices, buffers, ready):
            copy.start()

    for copy in weight_tiles(step, matrices, buffers, ready):
        copy.wait()


def forward_kernel(count, *refs):
    pieces, (slot, w_gate, w_up, rows_out, act, slope) = refs[:count], refs[count : count + 6]
    held, chosen, rows, sent = refs[count + 6 :]
    expert, tile = pl.program_id(0), pl.program_id(1)
    copy = pltpu.make_async_copy(rows, rows_out, sent)

    @pl.when((expert == 0) & (tile == 0))
    def _():
        dispatch(pieces, slot, held, chosen, rows)
        copy.start()

    x = rows[expert]
    gate = dot(x, w_gate[0])
    up = dot(x, w_up[0])
    sig = jax.nn.sigmoid(gate)
    act[0] = gate * sig
    slope[0] = up * sig * (1.0 + gate * (1.0 - sig))

    @pl.when((expert == pl.num_programs(0) - 1) & (tile == pl.num_programs(1) - 1))
    def _():
        copy.wait()


def forward(pieces, slot, w_gate, w_up):
    experts, blocks, tokens = slot.shape
    _, features, units = w_gate.shape
    tile = min(UNIT_TILE, units)
    slots = blocks * MOST
    matrix = pl.BlockSpec((1, features, tile), lambda l, f: (l, 0, f))
    unit = pl.BlockSpec((1, slots, tile), lambda l, f: (l, 0, f))
    return pl.pallas_call(
        functools.partial(forward_kernel, len(pieces)),
        grid=(experts, units // tile),
        in_specs=[whole(p.shape) for p in pieces] + [whole(slot.shape), matrix, matrix],
        out_specs=[pl.BlockSpec(memory_space=pltpu.HBM), unit, unit],
        out_shape=[
            jax.ShapeDtypeStruct((experts, slots, features), BF16),
            jax.ShapeDtypeStruct((experts, slots, units), F32),
            jax.ShapeDtypeStruct((experts, slots, units), F32),
        ],
        scratch_shapes=dispatch_scratch(experts, blocks, tokens, features)
        + [pltpu.SemaphoreType.DMA],
        compiler_params=params(2, 52),
        cost_estimate=pl.CostEstimate(
            flops=4 * experts * slots * features * units,
            bytes_accessed=4 * experts * features * units,
            transcendentals=experts * slots * units,
        ),
    )(*pieces, slot, w_gate, w_up)


def hidden_kernel(count, *refs):
    pieces, (slot, weight, act, slope, w_down) = refs[:count], refs[count : count + 5]
    gate_grad, up_grad, held, chosen, grads, downs, ready = refs[count + 5 :]
    step = pl.program_id(0)
    tiles = pl.num_programs(0) // grads.shape[0]
    fetching = ((w_down,), (downs,), ready)

    @pl.when(step == 0)
    def _():
        for first in weight_tiles(step, *fetching):
            first.start()
        dispatch(pieces, slot, held, chosen, grads, weight)

    next_tiles(step, *fetching)
    hidden = dot(grads[step // tiles], downs[step % 2])
    up_grad[0] = (hidden * act[0]).astype(BF16)
    gate_grad[0] = (hidden * slope[0]).astype(BF16)


def hidden_grads(pieces, slot, weight, act, slope, w_down):
    experts, blocks, tokens = slot.shape
    _, features, units = w_down.shape
    tile = min(UNIT_TILE, units)
    tiles = units // tile
    slots = blocks * MOST
    unit = pl.BlockSpec((1, slots, tile), lambda i: (i // tiles, 0, i % tiles))
    return pl.pallas_call(
        functools.partial(hidden_kernel, len(pieces)),
        grid=(experts * tiles,),
        in_specs=[whole(p.shape) for p in pieces]
        + [whole(slot.shape), whole(slot.shape), unit, unit, pl.BlockSpec(memory_space=pl.ANY)],
        out_specs=[unit, unit],
        out_shape=[jax.ShapeDtypeStruct((experts, slots, units), BF16)] * 2,
        scratch_shapes=dispatch_scratch(experts, blocks, tokens, features)
        + [pltpu.VMEM((2, features, tile), BF16), pltpu.SemaphoreType.DMA((2, 1))],
        compiler_params=params(1, 48),
        cost_estimate=pl.CostEstimate(
            flops=2 * experts * slots * features * units,
            bytes_accessed=2 * experts * features * units,
            transcendentals=0,
        ),
    )(*pieces, slot, weight, act, slope, w_down)


def inputs_kernel(groups, back, gate_grad, up_grad, w_gate, w_up, *refs):
    sums, held = refs[:-1], refs[-1]
    blocks, tokens, _ = back.shape
    for l in range(gate_grad.shape[0]):
        partial = dot(gate_grad[l], w_gate[l], NT) + dot(up_grad[l], w_up[l], NT)
        for b in range(blocks):
            held[b, l * MOST : (l + 1) * MOST] = partial[b * MOST : (b + 1) * MOST].astype(BF16)
    for out, members in zip(sums, groups):
        for place, b in enumerate(members):
            out[place * tokens : (place + 1) * tokens] = dot(back[b], held[b]).astype(BF16)


def input_sums(back, gate_grad, up_grad, w_gate, w_up, groups, part, parts):
    blocks, tokens, _ = back.shape
    experts, features, units = w_gate.shape
    wide = FEATURE_TILE
    steps = features // parts // wide
    slots = blocks * MOST
    across = pl.BlockSpec((experts, wide, units), lambda i: (0, part * steps + i, 0))
    return pl.pallas_call(
        functools.partial(inputs_kernel, groups),
        grid=(steps,),
        in_specs=[whole(back.shape), whole(gate_grad.shape), whole(up_grad.shape), across, across],
        out_specs=[pl.BlockSpec((len(g) * tokens, wide), lambda i: (0, i)) for g in groups],
        out_shape=[
            jax.ShapeDtypeStruct((len(g) * tokens, features // parts), BF16) for g in groups
        ],
        scratch_shapes=[pltpu.VMEM((blocks, experts * MOST, wide), BF16)],
        compiler_params=params(1, 40),
        cost_estimate=pl.CostEstimate(
            flops=4 * experts * slots * features * units // parts,
            bytes_accessed=4 * experts * features * units // parts,
            transcendentals=0,
        ),
    )(back, gate_grad, up_grad, w_gate, w_up)


def back_matrix(slot):
    places = jnp.arange(MOST, dtype=F32)
    slot = lax.optimization_barrier(slot.transpose(1, 2, 0))
    parts = [slot[..., l : l + 1] == places for l in range(slot.shape[2])]
    return jnp.concatenate([p.astype(BF16) for p in parts], axis=2)


def weights_kernel(rows, gate_grad, up_grad, *refs):
    grad_gate, grad_up = refs[-2:]
    grad_gate[0] = dot(rows[0], gate_grad[0], TN)
    grad_up[0] = dot(rows[0], up_grad[0], TN)


def weight_grads(rows, gate_grad, up_grad, before, first, steps):
    experts, slots, features = rows.shape
    units = gate_grad.shape[2]
    wide = FEATURE_TILE
    each = features // wide
    unit = pl.BlockSpec((1, slots, units), lambda i: ((first + i) // each, 0, 0))
    out = pl.BlockSpec((1, wide, units), lambda i: ((first + i) // each, (first + i) % each, 0))
    kept = [] if before is None else list(before)
    return pl.pallas_call(
        weights_kernel,
        grid=(steps,),
        in_specs=[
            pl.BlockSpec((1, slots, wide), lambda i: ((first + i) // each, 0, (first + i) % each)),
            unit,
            unit,
        ]
        + [pl.BlockSpec(memory_space=pl.ANY)] * len(kept),
        out_specs=[out, out],
        out_shape=[jax.ShapeDtypeStruct((experts, features, units), F32)] * 2,
        input_output_aliases={3 + i: i for i in range(len(kept))},
        compiler_params=params(1, 30),
        cost_estimate=pl.CostEstimate(
            flops=4 * slots * steps * wide * units,
            bytes_accessed=8 * steps * wide * units,
            transcendentals=0,
        ),
    )(rows, gate_grad, up_grad, *kept)


def route_table(routes, gate_values):
    tokens = routes.shape[0]
    experts = jnp.arange(EXPERTS, dtype=jnp.int32)[:, None, None]
    match = routes.T[None] == experts
    member = jnp.any(match, axis=1)
    gate = jnp.sum(jnp.where(match, gate_values.T[None], 0.0), axis=1)
    place = jnp.arange(tokens, dtype=jnp.int32)
    earlier = (place[:, None] < place[None, :]).astype(BF16)
    slot = jnp.where(member, dot(member.astype(BF16), earlier), -1.0)
    return jnp.stack([slot, gate], axis=1)


def flip(value, axis, bit):
    count = lax.axis_size(axis)
    return lax.ppermute(value, axis, [(i, i ^ bit) for i in range(count)])


def swap_order(value, side, pair, dim):
    shape = value.shape
    value = value.reshape(shape[:dim] + (2, 2, shape[dim] // 4) + shape[dim + 1 :])
    value = jnp.where(side == 1, jnp.flip(value, dim), value)
    return jnp.where(pair == 1, jnp.flip(value, dim + 1), value).reshape(shape)


def add(*terms):
    total = terms[0].astype(F32)
    for term in terms[1:]:
        total = total + term.astype(F32)
    return total.astype(BF16)


def quarters(value, count, at):
    return lax.dynamic_slice_in_dim(value, at * (count // 4), count // 4, 0)


def local_near(out_grad, routes, gate_values, layer_input, w_gate, w_up, w_down):
    experts, features, _ = w_gate.shape
    me = lax.axis_index("expert")
    position = lax.axis_index("dp")
    side, pair = position % 2, position // 2 % 2
    tokens = out_grad.shape[0]
    half, quarter = tokens // 2, tokens // 4
    corner = side * 2 + pair

    def to_core(values):
        return tuple(flip(v, "expert", 1) for v in values)

    x_mine = [quarters(layer_input, tokens, q) for q in (corner, 3 - corner)]
    *x_mine, layer_input, out_grad, routes = lax.optimization_barrier(
        (*x_mine, layer_input, out_grad, routes)
    )
    x_across, x_corner = [flip(v, "expert", 2) for v in x_mine]
    x_sibling, g_sibling = to_core((layer_input, out_grad))
    x_sibling, routes = lax.optimization_barrier((x_sibling, routes))
    table = route_table(routes, gate_values)
    tables = []
    for r in range(4):
        part = lax.dynamic_slice_in_dim(table, (me ^ r) * experts, experts, 0)
        tables.append(flip(part, "expert", r) if r > 0 else part)
    x_far = (x_across, x_corner, flip(x_across, "dp", 1), flip(x_across, "dp", 2))
    g_across = flip(out_grad, "expert", 2)
    x_far = (*x_far, *to_core(x_far))
    table = jnp.stack(tables, axis=2)
    slot, weight = table[:, 0], table[:, 1]
    back = back_matrix(swap_order(slot, side, pair, 2))
    far = swap_order(slot[:, 2:], side, pair, 2).reshape(experts, 2, 4, quarter)
    far = jnp.stack([far[:, :, q] for q in (0, 3, 2, 1)], axis=2).reshape(experts, 2, tokens)
    slot_x = jnp.concatenate([slot[:, :2], far], axis=1)
    slot_x, back = lax.optimization_barrier((slot_x, back))
    rows, act, slope = forward((layer_input, x_sibling, *x_far), slot_x, w_gate, w_up)
    act, g_across = lax.optimization_barrier((act, g_across))
    gate_grad, up_grad = hidden_grads(
        (out_grad, g_sibling, g_across, *to_core((g_across,))), slot, weight, act, slope, w_down
    )

    groups = ((0, 2), (1, 3))
    kept_a, sent_a = input_sums(back, gate_grad, up_grad, w_gate, w_up, groups, 0, 2)
    kept_b, sent_b = input_sums(back, gate_grad, up_grad, w_gate, w_up, groups, 1, 2)

    def piece(after, before, *which):
        held, rows_now = lax.optimization_barrier((after, rows))
        return held, weight_grads(rows_now, gate_grad, up_grad, before, *which)

    def corners(value):
        z, x, diagonal = value
        x, diagonal = flip(x, "dp", 1), flip(diagonal, "dp", 3)
        return [flip(z, "dp", 2), x, diagonal]

    def cut(value, count):
        return [value[i : i + quarter] for i in range(0, count * quarter, quarter)]

    chip_a = add(kept_a, flip(sent_a, "expert", 1))
    got = flip(sent_b, "expert", 1)
    chip_b = [add(a, b) for a, b in zip(cut(kept_b, 8), cut(got, 8))]
    far_a = chip_a[tokens:]
    away = [jnp.concatenate([chip_b[q], chip_b[4 + q]], axis=0) for q in (1, 2, 3)]
    (far_a, *away), grads = piece((far_a, *away), None, 0, 4)
    got_x = flip(away[1], "dp", 1)
    got_a = flip(far_a, "expert", 2)
    got_b = [flip(away[2], "dp", 3), flip(away[0], "dp", 2), got_x]
    got_a, got_b, *grads = lax.optimization_barrier((got_a, got_b, *grads))
    own_a = [add(a, b) for a, b in zip(cut(chip_a, 4), cut(got_a, 4))]
    mine_b = add(chip_b[0], *(v[:quarter] for v in got_b))
    far_b = add(chip_b[4], *(v[quarter:] for v in got_b))
    (far_b, *own_a), grads = piece((far_b, *own_a), grads, 4, 1)
    got_a, got_b = corners(own_a[1:]), flip(far_b, "expert", 2)
    got_a, got_b, *grads = lax.optimization_barrier((got_a, got_b, *grads))
    mine = jnp.concatenate([add(own_a[0], *got_a), add(mine_b, got_b)], axis=1)
    mine, grads = piece(mine, grads, 5, 4)
    got = flip(mine, "dp", 4)
    got, *grads = lax.optimization_barrier((got, *grads))
    mine = add(mine, got)
    mine, grads = piece(mine, grads, 9, 3)
    got = corners([mine] * 3)
    got, *grads = lax.optimization_barrier((got, *grads))
    total = swap_order(jnp.concatenate([mine, *got], axis=0), side, pair, 0)
    return (total, *grads)


def local_any(out_grad, routes, gate_values, layer_input, w_gate, w_up, w_down):
    experts = w_gate.shape[0]
    me = lax.axis_index("expert")
    rows_in = lax.all_gather(layer_input, "expert", tiled=True)
    grads_in = lax.all_gather(out_grad, "expert", tiled=True)
    table = lax.all_gather(route_table(routes, gate_values), "expert")
    table = lax.dynamic_slice_in_dim(table, me * experts, experts, 1).transpose(1, 2, 0, 3)
    slot, weight = table[:, 0], table[:, 1]
    rows, act, slope = forward([rows_in], slot, w_gate, w_up)
    gate_grad, up_grad = hidden_grads([grads_in], slot, weight, act, slope, w_down)
    groups = (tuple(range(slot.shape[1])),)
    (sums,) = input_sums(back_matrix(slot), gate_grad, up_grad, w_gate, w_up, groups, 0, 1)
    blocks = experts * layer_input.shape[1] // FEATURE_TILE
    grads = weight_grads(rows, gate_grad, up_grad, None, 0, blocks)
    own = lax.psum_scatter(sums, "expert", scatter_dimension=0, tiled=True)
    return (lax.psum(own, "dp"), *grads)


def solution(mesh):
    near = mesh.shape["dp"] == 8 and mesh.shape["expert"] == 4
    placed = (
        P("expert", None),
        P("expert", None),
        P("expert", None),
        P("expert", None),
        P("expert", None, "dp"),
        P("expert", None, "dp"),
        P("expert", None, "dp"),
    )
    return jax.shard_map(
        local_near if near else local_any,
        mesh=mesh,
        in_specs=placed,
        out_specs=(P("expert", None), P("expert", None, "dp"), P("expert", None, "dp")),
        check_vma=False,
    )
```

profile of v0, /device:TPU:0, one launch (start us, length us, event | category | flops | bytes accessed | tf_op | source)
XLA Modules:
  0.0 113.8 jit_solution(16655673677420335364)
XLA Ops:
  0.7 1.1 constant_dynamic-slice_fusion
  1.7 0.5 collective-permute-start
  2.3 2.6 %collective-permute-start.5 = (bf16[32,3072]{1,0:T(8,128)(2,1)S(1)}, bf16[32,3072]{1,0:T(8,128)(2,1)S(1)}, u32[]{:S(2)}, u32[]{:S(2)}) collective-permute-start(bf16[32,3072]{1,0:T(8,128)(2,1)S(1)} %get-tuple-element.72), channel_id=1, source_target_pairs={{0,2},{1,3},{2,0},{3,1},{4,6},{5,7},{6,4},{7,5},{8,10},{9,11},{10,... | collective-permute-start | bytes 589832 | tf_op jit(solution)/shard_map/ppermute | solution.py:301
  4.9 5.7 %collective-permute-done.5.refs_2_ = bf16[32,3072]{1,0:T(8,128)(2,1)S(1)} collective-permute-done((bf16[32,3072]{1,0:T(8,128)(2,1)S(1)}, bf16[32,3072]{1,0:T(8,128)(2,1)S(1)}, u32[]{:S(2)}, u32[]{:S(2)}) %collective-permute-start.5) | collective-permute-done | bytes 196640 | tf_op jit(solution)/shard_map/ppermute | solution.py:301
  10.6 2.0 %collective-permute-start.8 = (bf16[32,3072]{1,0:T(8,128)(2,1)S(1)}, bf16[32,3072]{1,0:T(8,128)(2,1)S(1)}, u32[]{:S(2)}, u32[]{:S(2)}) collective-permute-start(bf16[32,3072]{1,0:T(8,128)(2,1)S(1)} %collective-permute-done.5.refs_2_), channel_id=1, source_target_pairs={{0,8},{4,12},{8,0},{12,4},{16,24},{20,28},{24,16},{28,20},{1,9},{5... | collective-permute-start | bytes 589832 | tf_op jit(solution)/shard_map/ppermute | solution.py:301
  12.6 1.5 %collective-permute-start.7 = (bf16[32,3072]{1,0:T(8,128)(2,1)S(1)}, bf16[32,3072]{1,0:T(8,128)(2,1)S(1)}, u32[]{:S(2)}, u32[]{:S(2)}) collective-permute-start(bf16[32,3072]{1,0:T(8,128)(2,1)S(1)} %collective-permute-done.5.refs_2_), channel_id=1, source_target_pairs={{0,4},{4,0},{8,12},{12,8},{16,20},{20,16},{24,28},{28,24},{1,5},{5... | collective-permute-start | bytes 589832 | tf_op jit(solution)/shard_map/ppermute | solution.py:301
  14.1 0.7 fusion.1
  14.9 0.7 select_reduce_fusion
  15.7 1.6 %collective-permute-start.2 = (f32[2,2,128]{2,0,1:T(2,128)S(1)}, f32[2,2,128]{2,0,1:T(2,128)S(1)}, u32[]{:S(2)}, u32[]{:S(2)}) collective-permute-start(f32[2,2,128]{2,0,1:T(2,128)S(1)} %get-tuple-element.150), channel_id=1, source_target_pairs={{0,2},{1,3},{2,0},{3,1},{4,6},{5,7},{6,4},{7,5},{8,10},{9,11},{10,... | collective-permute-start | bytes 6152 | tf_op jit(solution)/shard_map/ppermute | solution.py:301
  17.3 0.3 collective-permute-start.3
  17.6 1.5 %collective-permute-start.13 = (bf16[128,3072]{1,0:T(8,128)(2,1)}, bf16[128,3072]{1,0:T(8,128)(2,1)S(1)}, u32[]{:S(2)}, u32[]{:S(2)}) collective-permute-start(bf16[128,3072]{1,0:T(8,128)(2,1)} %refs_0_.1), channel_id=1, source_target_pairs={{0,2},{1,3},{2,0},{3,1},{4,6},{5,7},{6,4},{7,5},{8,10},{9,11},{10,... | collective-permute-start | bytes 2359304 | tf_op jit(solution)/shard_map/ppermute | solution.py:301
  19.2 0.4 collective-permute-start.10
  19.7 0.6 collective-permute-done.3
  21.1 0.2 iota_compare_fusion
  21.3 0.2 add_convert_fusion.1.back
  21.5 0.4 collective-permute-start.4
  22.0 15.9 %shard_map.94 = (bf16[2,320,3072]{2,1,0:T(8,128)(2,1)}, f32[2,320,1024]{2,1,0:T(8,128)}, f32[2,320,1024]{2,1,0:T(8,128)}) custom-call(bf16[128,3072]{1,0:T(8,128)(2,1)} %refs_0_, bf16[128,3072]{1,0:T(8,128)(2,1)} %copy-done.2, bf16[32,3072]{1,0:T(8,128)(2,1)S(1)} %collective-permute-done.5.refs_2_, bf16[32,3072]{1,0:T(8,128)(2,1)S(1)} %collective-permute-done.6.refs_3_, ...), custom_call_target="tpu_custom_call" | custom-call | flops 8053063680 | bytes 25165824 | tf_op jit(solution)/shard_map/pallas_call | solution.py:143
  37.9 0.2 collective-permute-start.14
  38.1 2.1 %collective-permute-done.14.refs_3_ = bf16[128,3072]{1,0:T(8,128)(2,1)S(1)} collective-permute-done((bf16[128,3072]{1,0:T(8,128)(2,1)S(1)}, bf16[128,3072]{1,0:T(8,128)(2,1)S(1)}, u32[]{:S(2)}, u32[]{:S(2)}) %collective-permute-start.14) | collective-permute-done | bytes 786464 | tf_op jit(solution)/shard_map/ppermute | solution.py:301
  40.3 9.6 %shard_map.95 = (bf16[2,320,1024]{2,1,0:T(8,128)(2,1)S(1)}, bf16[2,320,1024]{2,1,0:T(8,128)(2,1)S(1)}) custom-call(bf16[128,3072]{1,0:T(8,128)(2,1)S(1)} %copy-done.1, bf16[128,3072]{1,0:T(8,128)(2,1)S(1)} %collective-permute-done.4.refs_1_, bf16[128,3072]{1,0:T(8,128)(2,1)S(1)} %collective-permute-done.13.refs_2_, ...), custom_call_target="tpu_custom_call" | custom-call | flops 4026531840 | bytes 12582912 | tf_op jit(solution)/shard_map/pallas_call | solution.py:190
  49.9 8.1 %shard_map.97 = (bf16[256,1536]{1,0:T(8,128)(2,1)S(1)}, bf16[256,1536]{1,0:T(8,128)(2,1)S(1)}) custom-call(bf16[4,128,160]{2,1,0:T(8,128)(2,1)S(1)} %add_convert_fusion.1.back, bf16[2,320,1024]{2,1,0:T(8,128)(2,1)S(1)} %get-tuple-element.79.gate_grad, bf16[2,320,1024]{2,1,0:T(8,128)(2,1)S(1)} %get-tuple-element.80.up_grad, bf16[2,3072,1024]{2,1,0:T(8,128)(2,1)} %w_gate.3, ...), custom_call_target="tpu_custom_call" | custom-call | flops 4026531840 | bytes 12582912 | tf_op jit(solution)/shard_map/pallas_call | solution.py:227
  58.0 0.2 collective-permute-start.16
  58.2 8.1 %shard_map.96 = (bf16[256,1536]{1,0:T(8,128)(2,1)S(1)}, bf16[256,1536]{1,0:T(8,128)(2,1)S(1)}) custom-call(bf16[4,128,160]{2,1,0:T(8,128)(2,1)S(1)} %add_convert_fusion.1.back, bf16[2,320,1024]{2,1,0:T(8,128)(2,1)S(1)} %get-tuple-element.79.gate_grad, bf16[2,320,1024]{2,1,0:T(8,128)(2,1)S(1)} %get-tuple-element.80.up_grad, bf16[2,3072,1024]{2,1,0:T(8,128)(2,1)} %w_gate.3, ...), custom_call_target="tpu_custom_call" | custom-call | flops 4026531840 | bytes 12582912 | tf_op jit(solution)/shard_map/pallas_call | solution.py:227
  66.4 0.4 collective-permute-start.15
  67.0 1.7 %collective-permute-done.15 = bf16[256,1536]{1,0:T(8,128)(2,1)S(1)} collective-permute-done((bf16[256,1536]{1,0:T(8,128)(2,1)S(1)}, bf16[256,1536]{1,0:T(8,128)(2,1)S(1)}, u32[]{:S(2)}, u32[]{:S(2)}) %collective-permute-start.15) | collective-permute-done | bytes 786464 | tf_op jit(solution)/shard_map/ppermute | solution.py:301
  68.9 1.2 %collective-permute-start.17 = (bf16[128,1536]{1,0:T(8,128)(2,1)S(1)}, bf16[128,1536]{1,0:T(8,128)(2,1)S(1)}, u32[]{:S(2)}, u32[]{:S(2)}) collective-permute-start(bf16[128,1536]{1,0:T(8,128)(2,1)S(1)} %slice.175), channel_id=1, source_target_pairs={{0,2},{1,3},{2,0},{3,1},{4,6},{5,7},{6,4},{7,5},{8,10},{9,11},{10,... | collective-permute-start | bytes 1179656 | tf_op jit(solution)/shard_map/ppermute | solution.py:301
  70.1 1.0 collective-permute-start.18
  71.1 1.2 %collective-permute-start.19 = (bf16[64,1536]{1,0:T(8,128)(2,1)S(1)}, bf16[64,1536]{1,0:T(8,128)(2,1)S(1)}, u32[]{:S(2)}, u32[]{:S(2)}) collective-permute-start(bf16[64,1536]{1,0:T(8,128)(2,1)S(1)} %pad_maximum_fusion.1), channel_id=1, source_target_pairs={{0,8},{4,12},{8,0},{12,4},{16,24},{20,28},{24,16},{28,20},{1,9},{5... | collective-permute-start | bytes 589832 | tf_op jit(solution)/shard_map/ppermute | solution.py:301
  72.3 1.3 %collective-permute-start.20 = (bf16[64,1536]{1,0:T(8,128)(2,1)S(1)}, bf16[64,1536]{1,0:T(8,128)(2,1)S(1)}, u32[]{:S(2)}, u32[]{:S(2)}) collective-permute-start(bf16[64,1536]{1,0:T(8,128)(2,1)S(1)} %pad_maximum_fusion.2), channel_id=1, source_target_pairs={{0,4},{4,0},{8,12},{12,8},{16,20},{20,16},{24,28},{28,24},{1,5},{5... | collective-permute-start | bytes 589832 | tf_op jit(solution)/shard_map/ppermute | solution.py:301
  73.6 6.8 %shard_map.98 = (f32[2,3072,1024]{2,1,0:T(8,128)}, f32[2,3072,1024]{2,1,0:T(8,128)}) custom-call(bf16[2,320,3072]{2,1,0:T(8,128)(2,1)S(1)} %copy-done, bf16[2,320,1024]{2,1,0:T(8,128)(2,1)S(1)} %get-tuple-element.79.gate_grad, bf16[2,320,1024]{2,1,0:T(8,128)(2,1)S(1)} %get-tuple-element.80.up_grad), custom_call_target="tpu_custom_call" | custom-call | flops 2684354560 | bytes 16777216 | tf_op jit(solution)/shard_map/pallas_call | solution.py:266
  80.5 0.7 collective-permute-done.19
  81.2 0.9 collective-permute-done.20
  82.3 0.5 collective-permute-start.21
  82.8 0.9 collective-permute-start.22
  83.7 2.2 %collective-permute-start.23 = (bf16[32,1536]{1,0:T(8,128)(2,1)S(1)}, bf16[32,1536]{1,0:T(8,128)(2,1)S(1)}, u32[]{:S(2)}, u32[]{:S(2)}) collective-permute-start(bf16[32,1536]{1,0:T(8,128)(2,1)S(1)} %get-tuple-element.100), channel_id=1, source_target_pairs={{0,12},{4,8},{8,4},{12,0},{16,28},{20,24},{24,20},{28,16},{1,13},{... | collective-permute-start | bytes 294920 | tf_op jit(solution)/shard_map/ppermute | solution.py:301
  85.9 0.9 collective-permute-start.24
  86.7 2.8 %shard_map.99 = (f32[2,3072,1024]{2,1,0:T(8,128)}, f32[2,3072,1024]{2,1,0:T(8,128)}) custom-call(bf16[2,320,3072]{2,1,0:T(8,128)(2,1)S(1)} %copy-done, bf16[2,320,1024]{2,1,0:T(8,128)(2,1)S(1)} %get-tuple-element.79.gate_grad, bf16[2,320,1024]{2,1,0:T(8,128)(2,1)S(1)} %get-tuple-element.80.up_grad, ...), custom_call_target="tpu_custom_call", output_to_operand_aliasing={{0}: (3, {}), {1}: (4, {})} | custom-call | flops 671088640 | bytes 4194304 | tf_op jit(solution)/shard_map/pallas_call | solution.py:266
  89.6 0.9 collective-permute-done.24
  90.6 2.7 %collective-permute-start.25 = (bf16[32,3072]{1,0:T(8,128)(2,1)S(1)}, bf16[32,3072]{1,0:T(8,128)(2,1)S(1)}, u32[]{:S(2)}, u32[]{:S(2)}) collective-permute-start(bf16[32,3072]{1,0:T(8,128)(2,1)S(1)} %pad_maximum_fusion.4), channel_id=1, source_target_pairs={{0,16},{4,20},{8,24},{12,28},{16,0},{20,4},{24,8},{28,12},{1,17},{... | collective-permute-start | bytes 589832 | tf_op jit(solution)/shard_map/ppermute | solution.py:301
  93.3 6.8 %shard_map.100 = (f32[2,3072,1024]{2,1,0:T(8,128)}, f32[2,3072,1024]{2,1,0:T(8,128)}) custom-call(bf16[2,320,3072]{2,1,0:T(8,128)(2,1)S(1)} %copy-done, bf16[2,320,1024]{2,1,0:T(8,128)(2,1)S(1)} %get-tuple-element.79.gate_grad, bf16[2,320,1024]{2,1,0:T(8,128)(2,1)S(1)} %get-tuple-element.80.up_grad, ...), custom_call_target="tpu_custom_call", output_to_operand_aliasing={{0}: (3, {}), {1}: (4, {})} | custom-call | flops 2684354560 | bytes 16777216 | tf_op jit(solution)/shard_map/pallas_call | solution.py:266
  100.1 0.7 collective-permute-done.25
  100.9 0.4 collective-permute-start.28
  101.3 1.0 collective-permute-start.27
  102.3 2.1 %collective-permute-start.26 = (bf16[32,3072]{1,0:T(8,128)(2,1)S(1)}, bf16[32,3072]{1,0:T(8,128)(2,1)S(1)}, u32[]{:S(2)}, u32[]{:S(2)}) collective-permute-start(bf16[32,3072]{1,0:T(8,128)(2,1)S(1)} %add_convert_fusion.2), channel_id=1, source_target_pairs={{0,8},{4,12},{8,0},{12,4},{16,24},{20,28},{24,16},{28,20},{1,9},{5... | collective-permute-start | bytes 589832 | tf_op jit(solution)/shard_map/ppermute | solution.py:301
  104.4 5.5 %shard_map.101 = (f32[2,3072,1024]{2,1,0:T(8,128)}, f32[2,3072,1024]{2,1,0:T(8,128)}) custom-call(bf16[2,320,3072]{2,1,0:T(8,128)(2,1)S(1)} %copy-done, bf16[2,320,1024]{2,1,0:T(8,128)(2,1)S(1)} %get-tuple-element.79.gate_grad, bf16[2,320,1024]{2,1,0:T(8,128)(2,1)S(1)} %get-tuple-element.80.up_grad, ...), custom_call_target="tpu_custom_call", output_to_operand_aliasing={{0}: (3, {}), {1}: (4, {})} | custom-call | flops 2013265920 | bytes 12582912 | tf_op jit(solution)/shard_map/pallas_call | solution.py:266
  110.0 1.5 %collective-permute-done.27 = bf16[32,3072]{1,0:T(8,128)(2,1)S(1)} collective-permute-done((bf16[32,3072]{1,0:T(8,128)(2,1)S(1)}, bf16[32,3072]{1,0:T(8,128)(2,1)S(1)}, u32[]{:S(2)}, u32[]{:S(2)}) %collective-permute-start.27) | collective-permute-done | bytes 196640 | tf_op jit(solution)/shard_map/ppermute | solution.py:301
  111.5 1.1 collective-permute-done.26
  112.8 1.0 reverse_select_fusion
  (63 shorter events, 2.2 us)
Async XLA Ops:
  1.7 12.4 %collective-permute-start = (bf16[128,3072]{1,0:T(8,128)(2,1)}, bf16[128,3072]{1,0:T(8,128)(2,1)S(1)}, u32[]{:S(2)}, u32[]{:S(2)}) collective-permute-start(bf16[128,3072]{1,0:T(8,128)(2,1)} %refs_0_), channel_id=1, source_target_pairs={{0,1},{1,0},{2,3},{3,2},{4,5},{5,4},{6,7},{7,6},{8,9},{9,8},{10,11... | collective-permute-start | bytes 2359304 | tf_op jit(solution)/shard_map/ppermute | solution.py:301
  2.3 8.4 %collective-permute-start.5 = (bf16[32,3072]{1,0:T(8,128)(2,1)S(1)}, bf16[32,3072]{1,0:T(8,128)(2,1)S(1)}, u32[]{:S(2)}, u32[]{:S(2)}) collective-permute-start(bf16[32,3072]{1,0:T(8,128)(2,1)S(1)} %get-tuple-element.72), channel_id=1, source_target_pairs={{0,2},{1,3},{2,0},{3,1},{4,6},{5,7},{6,4},{7,5},{8,10},{9,11},{10,... | collective-permute-start | bytes 589832 | tf_op jit(solution)/shard_map/ppermute | solution.py:301
  4.8 12.5 %collective-permute-start.6 = (bf16[32,3072]{1,0:T(8,128)(2,1)S(1)}, bf16[32,3072]{1,0:T(8,128)(2,1)S(1)}, u32[]{:S(2)}, u32[]{:S(2)}) collective-permute-start(bf16[32,3072]{1,0:T(8,128)(2,1)S(1)} %get-tuple-element.73), channel_id=1, source_target_pairs={{0,2},{1,3},{2,0},{3,1},{4,6},{5,7},{6,4},{7,5},{8,10},{9,11},{10,... | collective-permute-start | bytes 589832 | tf_op jit(solution)/shard_map/ppermute | solution.py:301
  10.6 7.0 %collective-permute-start.8 = (bf16[32,3072]{1,0:T(8,128)(2,1)S(1)}, bf16[32,3072]{1,0:T(8,128)(2,1)S(1)}, u32[]{:S(2)}, u32[]{:S(2)}) collective-permute-start(bf16[32,3072]{1,0:T(8,128)(2,1)S(1)} %collective-permute-done.5.refs_2_), channel_id=1, source_target_pairs={{0,8},{4,12},{8,0},{12,4},{16,24},{20,28},{24,16},{28,20},{1,9},{5... | collective-permute-start | bytes 589832 | tf_op jit(solution)/shard_map/ppermute | solution.py:301
  12.6 6.5 %collective-permute-start.7 = (bf16[32,3072]{1,0:T(8,128)(2,1)S(1)}, bf16[32,3072]{1,0:T(8,128)(2,1)S(1)}, u32[]{:S(2)}, u32[]{:S(2)}) collective-permute-start(bf16[32,3072]{1,0:T(8,128)(2,1)S(1)} %collective-permute-done.5.refs_2_), channel_id=1, source_target_pairs={{0,4},{4,0},{8,12},{12,8},{16,20},{20,16},{24,28},{28,24},{1,5},{5... | collective-permute-start | bytes 589832 | tf_op jit(solution)/shard_map/ppermute | solution.py:301
  14.1 7.9 %copy-start.2 = (bf16[128,3072]{1,0:T(8,128)(2,1)}, bf16[128,3072]{1,0:T(8,128)(2,1)S(1)}, u32[]{:S(2)}) copy-start(bf16[128,3072]{1,0:T(8,128)(2,1)S(1)} %collective-permute-done.refs_1_) | copy-start | bytes 2359300
  15.6 3.5 %collective-permute-start.1 = (f32[2,2,128]{2,0,1:T(2,128)S(1)}, f32[2,2,128]{2,0,1:T(2,128)S(1)}, u32[]{:S(2)}, u32[]{:S(2)}) collective-permute-start(f32[2,2,128]{2,0,1:T(2,128)S(1)} %get-tuple-element.149), channel_id=1, source_target_pairs={{0,1},{1,0},{2,3},{3,2},{4,5},{5,4},{6,7},{7,6},{8,9},{9,8},{10,11... | collective-permute-start | bytes 6152 | tf_op jit(solution)/shard_map/ppermute | solution.py:301
  15.7 3.9 %collective-permute-start.2 = (f32[2,2,128]{2,0,1:T(2,128)S(1)}, f32[2,2,128]{2,0,1:T(2,128)S(1)}, u32[]{:S(2)}, u32[]{:S(2)}) collective-permute-start(f32[2,2,128]{2,0,1:T(2,128)S(1)} %get-tuple-element.150), channel_id=1, source_target_pairs={{0,2},{1,3},{2,0},{3,1},{4,6},{5,7},{6,4},{7,5},{8,10},{9,11},{10,... | collective-permute-start | bytes 6152 | tf_op jit(solution)/shard_map/ppermute | solution.py:301
  17.3 3.0 %collective-permute-start.3 = (f32[2,2,128]{2,0,1:T(2,128)S(1)}, f32[2,2,128]{2,0,1:T(2,128)S(1)}, u32[]{:S(2)}, u32[]{:S(2)}) collective-permute-start(f32[2,2,128]{2,0,1:T(2,128)S(1)} %get-tuple-element.151), channel_id=1, source_target_pairs={{0,3},{1,2},{2,1},{3,0},{4,7},{5,6},{6,5},{7,4},{8,11},{9,10},{10,... | collective-permute-start | bytes 6152 | tf_op jit(solution)/shard_map/ppermute | solution.py:301
  17.6 20.3 %collective-permute-start.13 = (bf16[128,3072]{1,0:T(8,128)(2,1)}, bf16[128,3072]{1,0:T(8,128)(2,1)S(1)}, u32[]{:S(2)}, u32[]{:S(2)}) collective-permute-start(bf16[128,3072]{1,0:T(8,128)(2,1)} %refs_0_.1), channel_id=1, source_target_pairs={{0,2},{1,3},{2,0},{3,1},{4,6},{5,7},{6,4},{7,5},{8,10},{9,11},{10,... | collective-permute-start | bytes 2359304 | tf_op jit(solution)/shard_map/ppermute | solution.py:301
  19.1 2.4 %collective-permute-start.9 = (bf16[32,3072]{1,0:T(8,128)(2,1)S(1)}, bf16[32,3072]{1,0:T(8,128)(2,1)S(1)}, u32[]{:S(2)}, u32[]{:S(2)}) collective-permute-start(bf16[32,3072]{1,0:T(8,128)(2,1)S(1)} %collective-permute-done.5.refs_2_), channel_id=1, source_target_pairs={{0,1},{1,0},{2,3},{3,2},{4,5},{5,4},{6,7},{7,6},{8,9},{9,8},{10,11... | collective-permute-start | bytes 589832 | tf_op jit(solution)/shard_map/ppermute | solution.py:301
  19.2 2.8 %collective-permute-start.10 = (bf16[32,3072]{1,0:T(8,128)(2,1)S(1)}, bf16[32,3072]{1,0:T(8,128)(2,1)S(1)}, u32[]{:S(2)}, u32[]{:S(2)}) collective-permute-start(bf16[32,3072]{1,0:T(8,128)(2,1)S(1)} %collective-permute-done.6.refs_3_), channel_id=1, source_target_pairs={{0,1},{1,0},{2,3},{3,2},{4,5},{5,4},{6,7},{7,6},{8,9},{9,8},{10,11... | collective-permute-start | bytes 589832 | tf_op jit(solution)/shard_map/ppermute | solution.py:301
  19.6 2.3 %collective-permute-start.12 = (bf16[32,3072]{1,0:T(8,128)(2,1)S(1)}, bf16[32,3072]{1,0:T(8,128)(2,1)S(1)}, u32[]{:S(2)}, u32[]{:S(2)}) collective-permute-start(bf16[32,3072]{1,0:T(8,128)(2,1)S(1)} %collective-permute-done.8.refs_5_), channel_id=1, source_target_pairs={{0,1},{1,0},{2,3},{3,2},{4,5},{5,4},{6,7},{7,6},{8,9},{9,8},{10,11... | collective-permute-start | bytes 589832 | tf_op jit(solution)/shard_map/ppermute | solution.py:301
  20.3 1.6 %collective-permute-start.11 = (bf16[32,3072]{1,0:T(8,128)(2,1)S(1)}, bf16[32,3072]{1,0:T(8,128)(2,1)S(1)}, u32[]{:S(2)}, u32[]{:S(2)}) collective-permute-start(bf16[32,3072]{1,0:T(8,128)(2,1)S(1)} %collective-permute-done.7.refs_4_), channel_id=1, source_target_pairs={{0,1},{1,0},{2,3},{3,2},{4,5},{5,4},{6,7},{7,6},{8,9},{9,8},{10,11... | collective-permute-start | bytes 589832 | tf_op jit(solution)/shard_map/ppermute | solution.py:301
  21.5 18.7 %copy-start.1 = (bf16[128,3072]{1,0:T(8,128)(2,1)S(1)}, bf16[128,3072]{1,0:T(8,128)(2,1)}, u32[]{:S(2)}) copy-start(bf16[128,3072]{1,0:T(8,128)(2,1)} %refs_0_.1) | copy-start | bytes 2359300
  21.5 16.6 %collective-permute-start.4 = (bf16[128,3072]{1,0:T(8,128)(2,1)}, bf16[128,3072]{1,0:T(8,128)(2,1)S(1)}, u32[]{:S(2)}, u32[]{:S(2)}) collective-permute-start(bf16[128,3072]{1,0:T(8,128)(2,1)} %refs_0_.1), channel_id=1, source_target_pairs={{0,1},{1,0},{2,3},{3,2},{4,5},{5,4},{6,7},{7,6},{8,9},{9,8},{10,11... | collective-permute-start | bytes 2359304 | tf_op jit(solution)/shard_map/ppermute | solution.py:301
  37.9 2.4 %collective-permute-start.14 = (bf16[128,3072]{1,0:T(8,128)(2,1)S(1)}, bf16[128,3072]{1,0:T(8,128)(2,1)S(1)}, u32[]{:S(2)}, u32[]{:S(2)}) collective-permute-start(bf16[128,3072]{1,0:T(8,128)(2,1)S(1)} %collective-permute-done.13.refs_2_), channel_id=1, source_target_pairs={{0,1},{1,0},{2,3},{3,2},{4,5},{5,4},{6,7},{7,6},{8,9},{9,8},{10,11... | collective-permute-start | bytes 2359304 | tf_op jit(solution)/shard_map/ppermute | solution.py:301
  58.0 8.8 %collective-permute-start.16 = (bf16[256,1536]{1,0:T(8,128)(2,1)S(1)}, bf16[256,1536]{1,0:T(8,128)(2,1)S(1)}, u32[]{:S(2)}, u32[]{:S(2)}) collective-permute-start(bf16[256,1536]{1,0:T(8,128)(2,1)S(1)} %get-tuple-element.84), channel_id=1, source_target_pairs={{0,1},{1,0},{2,3},{3,2},{4,5},{5,4},{6,7},{7,6},{8,9},{9,8},{10,11... | collective-permute-start | bytes 2359304 | tf_op jit(solution)/shard_map/ppermute | solution.py:301
  66.4 2.4 %collective-permute-start.15 = (bf16[256,1536]{1,0:T(8,128)(2,1)S(1)}, bf16[256,1536]{1,0:T(8,128)(2,1)S(1)}, u32[]{:S(2)}, u32[]{:S(2)}) collective-permute-start(bf16[256,1536]{1,0:T(8,128)(2,1)S(1)} %get-tuple-element.82), channel_id=1, source_target_pairs={{0,1},{1,0},{2,3},{3,2},{4,5},{5,4},{6,7},{7,6},{8,9},{9,8},{10,11... | collective-permute-start | bytes 2359304 | tf_op jit(solution)/shard_map/ppermute | solution.py:301
  66.8 6.8 %copy-start = (bf16[2,320,3072]{2,1,0:T(8,128)(2,1)S(1)}, bf16[2,320,3072]{2,1,0:T(8,128)(2,1)}, u32[]{:S(2)}) copy-start(bf16[2,320,3072]{2,1,0:T(8,128)(2,1)} %get-tuple-element.119.rows) | copy-start | bytes 11796484
  68.9 13.2 %collective-permute-start.17 = (bf16[128,1536]{1,0:T(8,128)(2,1)S(1)}, bf16[128,1536]{1,0:T(8,128)(2,1)S(1)}, u32[]{:S(2)}, u32[]{:S(2)}) collective-permute-start(bf16[128,1536]{1,0:T(8,128)(2,1)S(1)} %slice.175), channel_id=1, source_target_pairs={{0,2},{1,3},{2,0},{3,1},{4,6},{5,7},{6,4},{7,5},{8,10},{9,11},{10,... | collective-permute-start | bytes 1179656 | tf_op jit(solution)/shard_map/ppermute | solution.py:301
  70.1 10.3 %collective-permute-start.18 = (bf16[64,1536]{1,0:T(8,128)(2,1)S(1)}, bf16[64,1536]{1,0:T(8,128)(2,1)S(1)}, u32[]{:S(2)}, u32[]{:S(2)}) collective-permute-start(bf16[64,1536]{1,0:T(8,128)(2,1)S(1)} %pad_maximum_fusion.3), channel_id=1, source_target_pairs={{0,12},{4,8},{8,4},{12,0},{16,28},{20,24},{24,20},{28,16},{1,13},{... | collective-permute-start | bytes 589832 | tf_op jit(solution)/shard_map/ppermute | solution.py:301
  71.1 10.1 %collective-permute-start.19 = (bf16[64,1536]{1,0:T(8,128)(2,1)S(1)}, bf16[64,1536]{1,0:T(8,128)(2,1)S(1)}, u32[]{:S(2)}, u32[]{:S(2)}) collective-permute-start(bf16[64,1536]{1,0:T(8,128)(2,1)S(1)} %pad_maximum_fusion.1), channel_id=1, source_target_pairs={{0,8},{4,12},{8,0},{12,4},{16,24},{20,28},{24,16},{28,20},{1,9},{5... | collective-permute-start | bytes 589832 | tf_op jit(solution)/shard_map/ppermute | solution.py:301
  72.3 9.8 %collective-permute-start.20 = (bf16[64,1536]{1,0:T(8,128)(2,1)S(1)}, bf16[64,1536]{1,0:T(8,128)(2,1)S(1)}, u32[]{:S(2)}, u32[]{:S(2)}) collective-permute-start(bf16[64,1536]{1,0:T(8,128)(2,1)S(1)} %pad_maximum_fusion.2), channel_id=1, source_target_pairs={{0,4},{4,0},{8,12},{12,8},{16,20},{20,16},{24,28},{28,24},{1,5},{5... | collective-permute-start | bytes 589832 | tf_op jit(solution)/shard_map/ppermute | solution.py:301
  82.3 7.2 %collective-permute-start.21 = (bf16[32,1536]{1,0:T(8,128)(2,1)S(1)}, bf16[32,1536]{1,0:T(8,128)(2,1)S(1)}, u32[]{:S(2)}, u32[]{:S(2)}) collective-permute-start(bf16[32,1536]{1,0:T(8,128)(2,1)S(1)} %get-tuple-element.98), channel_id=1, source_target_pairs={{0,8},{4,12},{8,0},{12,4},{16,24},{20,28},{24,16},{28,20},{1,9},{5... | collective-permute-start | bytes 294920 | tf_op jit(solution)/shard_map/ppermute | solution.py:301
  82.8 6.7 %collective-permute-start.22 = (bf16[32,1536]{1,0:T(8,128)(2,1)S(1)}, bf16[32,1536]{1,0:T(8,128)(2,1)S(1)}, u32[]{:S(2)}, u32[]{:S(2)}) collective-permute-start(bf16[32,1536]{1,0:T(8,128)(2,1)S(1)} %get-tuple-element.99), channel_id=1, source_target_pairs={{0,4},{4,0},{8,12},{12,8},{16,20},{20,16},{24,28},{28,24},{1,5},{5... | collective-permute-start | bytes 294920 | tf_op jit(solution)/shard_map/ppermute | solution.py:301
  83.7 5.9 %collective-permute-start.23 = (bf16[32,1536]{1,0:T(8,128)(2,1)S(1)}, bf16[32,1536]{1,0:T(8,128)(2,1)S(1)}, u32[]{:S(2)}, u32[]{:S(2)}) collective-permute-start(bf16[32,1536]{1,0:T(8,128)(2,1)S(1)} %get-tuple-element.100), channel_id=1, source_target_pairs={{0,12},{4,8},{8,4},{12,0},{16,28},{20,24},{24,20},{28,16},{1,13},{... | collective-permute-start | bytes 294920 | tf_op jit(solution)/shard_map/ppermute | solution.py:301
  85.9 4.6 %collective-permute-start.24 = (bf16[32,1536]{1,0:T(8,128)(2,1)S(1)}, bf16[32,1536]{1,0:T(8,128)(2,1)S(1)}, u32[]{:S(2)}, u32[]{:S(2)}) collective-permute-start(bf16[32,1536]{1,0:T(8,128)(2,1)S(1)} %add_convert_fusion.11), channel_id=1, source_target_pairs={{0,2},{1,3},{2,0},{3,1},{4,6},{5,7},{6,4},{7,5},{8,10},{9,11},{10,... | collective-permute-start | bytes 294920 | tf_op jit(solution)/shard_map/ppermute | solution.py:301
  90.6 10.2 %collective-permute-start.25 = (bf16[32,3072]{1,0:T(8,128)(2,1)S(1)}, bf16[32,3072]{1,0:T(8,128)(2,1)S(1)}, u32[]{:S(2)}, u32[]{:S(2)}) collective-permute-start(bf16[32,3072]{1,0:T(8,128)(2,1)S(1)} %pad_maximum_fusion.4), channel_id=1, source_target_pairs={{0,16},{4,20},{8,24},{12,28},{16,0},{20,4},{24,8},{28,12},{1,17},{... | collective-permute-start | bytes 589832 | tf_op jit(solution)/shard_map/ppermute | solution.py:301
  100.9 9.1 %collective-permute-start.28 = (bf16[32,3072]{1,0:T(8,128)(2,1)S(1)}, bf16[32,3072]{1,0:T(8,128)(2,1)S(1)}, u32[]{:S(2)}, u32[]{:S(2)}) collective-permute-start(bf16[32,3072]{1,0:T(8,128)(2,1)S(1)} %add_convert_fusion.2), channel_id=1, source_target_pairs={{0,12},{4,8},{8,4},{12,0},{16,28},{20,24},{24,20},{28,16},{1,13},{... | collective-permute-start | bytes 589832 | tf_op jit(solution)/shard_map/ppermute | solution.py:301
  101.3 10.2 %collective-permute-start.27 = (bf16[32,3072]{1,0:T(8,128)(2,1)S(1)}, bf16[32,3072]{1,0:T(8,128)(2,1)S(1)}, u32[]{:S(2)}, u32[]{:S(2)}) collective-permute-start(bf16[32,3072]{1,0:T(8,128)(2,1)S(1)} %add_convert_fusion.2), channel_id=1, source_target_pairs={{0,4},{4,0},{8,12},{12,8},{16,20},{20,16},{24,28},{28,24},{1,5},{5... | collective-permute-start | bytes 589832 | tf_op jit(solution)/shard_map/ppermute | solution.py:301
  102.3 10.3 %collective-permute-start.26 = (bf16[32,3072]{1,0:T(8,128)(2,1)S(1)}, bf16[32,3072]{1,0:T(8,128)(2,1)S(1)}, u32[]{:S(2)}, u32[]{:S(2)}) collective-permute-start(bf16[32,3072]{1,0:T(8,128)(2,1)S(1)} %add_convert_fusion.2), channel_id=1, source_target_pairs={{0,8},{4,12},{8,0},{12,4},{16,24},{20,28},{24,16},{28,20},{1,9},{5... | collective-permute-start | bytes 589832 | tf_op jit(solution)/shard_map/ppermute | solution.py:301
where the time goes:
time: 114 us
  Pallas kernels  63.7 us (56%)
  starting transfers between devices  27.5 us (24%)
  waiting for transfers between devices  16.1 us (14%)
  other arithmetic  3.85 us (3%)
  local copies, waits for them, and re-layouts  1.54 us (1%)
    ppermute x29, starting transfers between devices, flip(): return lax.ppermute(value, axis, [(i, i ^ bit) for i in range(count)])  27.5 us
    pallas_call x4, Pallas kernels, weight_grads(): pl.pallas_call(weights_kernel, grid=(steps,), in_specs=[pl.BlockSpec((1,...  21.9 us
    pallas_call x2, Pallas kernels, input_sums(): pl.pallas_call(functools.partial(inputs_kernel, groups), grid=(steps,), i...  16.2 us
    ppermute x29, waiting for transfers between devices, flip(): return lax.ppermute(value, axis, [(i, i ^ bit) for i in range(count)])  16.1 us
    pallas_call x1, Pallas kernels, forward(): pl.pallas_call(functools.partial(forward_kernel, len(pieces)), grid=(expe...  15.9 us
    pallas_call x1, Pallas kernels, hidden_grads(): pl.pallas_call(functools.partial(hidden_kernel, len(pieces)), grid=(exper...  9.63 us
  transfers between devices with their start and end apart: 29, of which 11 were waited for; matrix products, arithmetic and copies ran while one was open for 2% of the time, Pallas kernels for 40%

commit v1 on v0

--- a/solution.py
+++ b/solution.py
@@ -378,11 +378,10 @@
     chip_a = add(kept_a, flip(sent_a, "expert", 1))
     got = flip(sent_b, "expert", 1)
     chip_b = [add(a, b) for a, b in zip(cut(kept_b, 8), cut(got, 8))]
-    far_a = chip_a[tokens:]
+    got_a = flip(chip_a[tokens:], "expert", 2)
     away = [jnp.concatenate([chip_b[q], chip_b[4 + q]], axis=0) for q in (1, 2, 3)]
-    (far_a, *away), grads = piece((far_a, *away), None, 0, 4)
+    away, grads = piece(away, None, 0, 4)
     got_x = flip(away[1], "dp", 1)
-    got_a = flip(far_a, "expert", 2)
     got_b = [flip(away[2], "dp", 3), flip(away[0], "dp", 2), got_x]
     got_a, got_b, *grads = lax.optimization_barrier((got_a, got_b, *grads))
     own_a = [add(a, b) for a, b in zip(cut(chip_a, 4), cut(got_a, 4))]

time: 114 us -> 113 us (level)
  waiting for transfers between devices: 16.1 us -> 14.5 us
    ppermute x29, waiting for transfers between devices: 16.1 us -> 14.5 us  [flip(): return lax.ppermute(value, axis, [(i, i ^ bit) for i in range(count)])]
  transfers between devices with their start and end apart: 29 -> 29, of which waited for: 11 -> 11; matrix products, arithmetic and copies ran while one was open for 2% -> 3% of each run, Pallas kernels for 40% -> 41%
where the time goes in v1:
time: 113 us
  Pallas kernels  63.7 us (56%)
  starting transfers between devices  27.9 us (25%)
  waiting for transfers between devices  14.5 us (13%)
  other arithmetic  3.85 us (3%)
  local copies, waits for them, and re-layouts  1.54 us (1%)
    ppermute x29, starting transfers between devices, flip(): return lax.ppermute(value, axis, [(i, i ^ bit) for i in range(count)])  27.9 us
    pallas_call x4, Pallas kernels, weight_grads(): pl.pallas_call(weights_kernel, grid=(steps,), in_specs=[pl.BlockSpec((1,...  22 us
    pallas_call x2, Pallas kernels, input_sums(): pl.pallas_call(functools.partial(inputs_kernel, groups), grid=(steps,), i...  16.2 us
    pallas_call x1, Pallas kernels, forward(): pl.pallas_call(functools.partial(forward_kernel, len(pieces)), grid=(expe...  15.9 us
    ppermute x29, waiting for transfers between devices, flip(): return lax.ppermute(value, axis, [(i, i ^ bit) for i in range(count)])  14.5 us
    pallas_call x1, Pallas kernels, hidden_grads(): pl.pallas_call(functools.partial(hidden_kernel, len(pieces)), grid=(exper...  9.63 us
  transfers between devices with their start and end apart: 29, of which 11 were waited for; matrix products, arithmetic and copies ran while one was open for 3% of the time, Pallas kernels for 41%

profile of v1, /device:TPU:0, one launch (start us, length us, event | category | flops | bytes accessed | tf_op | source)
XLA Modules:
  0.0 112.6 jit_solution(3673768248817211715)
XLA Ops:
  0.7 1.1 constant_dynamic-slice_fusion
  1.7 0.5 collective-permute-start
  2.3 2.6 %collective-permute-start.5 = (bf16[32,3072]{1,0:T(8,128)(2,1)S(1)}, bf16[32,3072]{1,0:T(8,128)(2,1)S(1)}, u32[]{:S(2)}, u32[]{:S(2)}) collective-permute-start(bf16[32,3072]{1,0:T(8,128)(2,1)S(1)} %get-tuple-element.71), channel_id=1, source_target_pairs={{0,2},{1,3},{2,0},{3,1},{4,6},{5,7},{6,4},{7,5},{8,10},{9,11},{10,... | collective-permute-start | bytes 589832 | tf_op jit(solution)/shard_map/ppermute | solution.py:301
  4.9 5.7 %collective-permute-done.5.refs_2_ = bf16[32,3072]{1,0:T(8,128)(2,1)S(1)} collective-permute-done((bf16[32,3072]{1,0:T(8,128)(2,1)S(1)}, bf16[32,3072]{1,0:T(8,128)(2,1)S(1)}, u32[]{:S(2)}, u32[]{:S(2)}) %collective-permute-start.5) | collective-permute-done | bytes 196640 | tf_op jit(solution)/shard_map/ppermute | solution.py:301
  10.6 2.0 %collective-permute-start.8 = (bf16[32,3072]{1,0:T(8,128)(2,1)S(1)}, bf16[32,3072]{1,0:T(8,128)(2,1)S(1)}, u32[]{:S(2)}, u32[]{:S(2)}) collective-permute-start(bf16[32,3072]{1,0:T(8,128)(2,1)S(1)} %collective-permute-done.5.refs_2_), channel_id=1, source_target_pairs={{0,8},{4,12},{8,0},{12,4},{16,24},{20,28},{24,16},{28,20},{1,9},{5... | collective-permute-start | bytes 589832 | tf_op jit(solution)/shard_map/ppermute | solution.py:301
  12.6 1.5 %collective-permute-start.7 = (bf16[32,3072]{1,0:T(8,128)(2,1)S(1)}, bf16[32,3072]{1,0:T(8,128)(2,1)S(1)}, u32[]{:S(2)}, u32[]{:S(2)}) collective-permute-start(bf16[32,3072]{1,0:T(8,128)(2,1)S(1)} %collective-permute-done.5.refs_2_), channel_id=1, source_target_pairs={{0,4},{4,0},{8,12},{12,8},{16,20},{20,16},{24,28},{28,24},{1,5},{5... | collective-permute-start | bytes 589832 | tf_op jit(solution)/shard_map/ppermute | solution.py:301
  14.1 0.7 fusion.1
  14.9 0.7 select_reduce_fusion
  15.7 1.6 %collective-permute-start.2 = (f32[2,2,128]{2,0,1:T(2,128)S(1)}, f32[2,2,128]{2,0,1:T(2,128)S(1)}, u32[]{:S(2)}, u32[]{:S(2)}) collective-permute-start(f32[2,2,128]{2,0,1:T(2,128)S(1)} %get-tuple-element.148), channel_id=1, source_target_pairs={{0,2},{1,3},{2,0},{3,1},{4,6},{5,7},{6,4},{7,5},{8,10},{9,11},{10,... | collective-permute-start | bytes 6152 | tf_op jit(solution)/shard_map/ppermute | solution.py:301
  17.3 0.3 collective-permute-start.3
  17.6 1.5 %collective-permute-start.13 = (bf16[128,3072]{1,0:T(8,128)(2,1)}, bf16[128,3072]{1,0:T(8,128)(2,1)S(1)}, u32[]{:S(2)}, u32[]{:S(2)}) collective-permute-start(bf16[128,3072]{1,0:T(8,128)(2,1)} %refs_0_.1), channel_id=1, source_target_pairs={{0,2},{1,3},{2,0},{3,1},{4,6},{5,7},{6,4},{7,5},{8,10},{9,11},{10,... | collective-permute-start | bytes 2359304 | tf_op jit(solution)/shard_map/ppermute | solution.py:301
  19.2 0.4 collective-permute-start.10
  19.7 0.6 collective-permute-done.3
  21.1 0.2 iota_compare_fusion
  21.3 0.2 add_convert_fusion.1.back
  21.5 0.4 collective-permute-start.4
  22.0 15.9 %shard_map.94 = (bf16[2,320,3072]{2,1,0:T(8,128)(2,1)}, f32[2,320,1024]{2,1,0:T(8,128)}, f32[2,320,1024]{2,1,0:T(8,128)}) custom-call(bf16[128,3072]{1,0:T(8,128)(2,1)} %refs_0_, bf16[128,3072]{1,0:T(8,128)(2,1)} %copy-done.2, bf16[32,3072]{1,0:T(8,128)(2,1)S(1)} %collective-permute-done.5.refs_2_, bf16[32,3072]{1,0:T(8,128)(2,1)S(1)} %collective-permute-done.6.refs_3_, ...), custom_call_target="tpu_custom_call" | custom-call | flops 8053063680 | bytes 25165824 | tf_op jit(solution)/shard_map/pallas_call | solution.py:143
  37.9 0.2 collective-permute-start.14
  38.1 2.1 %collective-permute-done.14.refs_3_ = bf16[128,3072]{1,0:T(8,128)(2,1)S(1)} collective-permute-done((bf16[128,3072]{1,0:T(8,128)(2,1)S(1)}, bf16[128,3072]{1,0:T(8,128)(2,1)S(1)}, u32[]{:S(2)}, u32[]{:S(2)}) %collective-permute-start.14) | collective-permute-done | bytes 786464 | tf_op jit(solution)/shard_map/ppermute | solution.py:301
  40.3 9.6 %shard_map.95 = (bf16[2,320,1024]{2,1,0:T(8,128)(2,1)S(1)}, bf16[2,320,1024]{2,1,0:T(8,128)(2,1)S(1)}) custom-call(bf16[128,3072]{1,0:T(8,128)(2,1)S(1)} %copy-done.1, bf16[128,3072]{1,0:T(8,128)(2,1)S(1)} %collective-permute-done.4.refs_1_, bf16[128,3072]{1,0:T(8,128)(2,1)S(1)} %collective-permute-done.13.refs_2_, ...), custom_call_target="tpu_custom_call" | custom-call | flops 4026531840 | bytes 12582912 | tf_op jit(solution)/shard_map/pallas_call | solution.py:190
  49.9 8.1 %shard_map.97 = (bf16[256,1536]{1,0:T(8,128)(2,1)S(1)}, bf16[256,1536]{1,0:T(8,128)(2,1)S(1)}) custom-call(bf16[4,128,160]{2,1,0:T(8,128)(2,1)S(1)} %add_convert_fusion.1.back, bf16[2,320,1024]{2,1,0:T(8,128)(2,1)S(1)} %get-tuple-element.78.gate_grad, bf16[2,320,1024]{2,1,0:T(8,128)(2,1)S(1)} %get-tuple-element.79.up_grad, bf16[2,3072,1024]{2,1,0:T(8,128)(2,1)} %w_gate.3, ...), custom_call_target="tpu_custom_call" | custom-call | flops 4026531840 | bytes 12582912 | tf_op jit(solution)/shard_map/pallas_call | solution.py:227
  58.0 0.2 collective-permute-start.16
  58.2 8.1 %shard_map.96 = (bf16[256,1536]{1,0:T(8,128)(2,1)S(1)}, bf16[256,1536]{1,0:T(8,128)(2,1)S(1)}) custom-call(bf16[4,128,160]{2,1,0:T(8,128)(2,1)S(1)} %add_convert_fusion.1.back, bf16[2,320,1024]{2,1,0:T(8,128)(2,1)S(1)} %get-tuple-element.78.gate_grad, bf16[2,320,1024]{2,1,0:T(8,128)(2,1)S(1)} %get-tuple-element.79.up_grad, bf16[2,3072,1024]{2,1,0:T(8,128)(2,1)} %w_gate.3, ...), custom_call_target="tpu_custom_call" | custom-call | flops 4026531840 | bytes 12582912 | tf_op jit(solution)/shard_map/pallas_call | solution.py:227
  66.4 0.4 collective-permute-start.15
  67.0 1.2 %collective-permute-start.17 = (bf16[128,1536]{1,0:T(8,128)(2,1)S(1)}, bf16[128,1536]{1,0:T(8,128)(2,1)S(1)}, u32[]{:S(2)}, u32[]{:S(2)}) collective-permute-start(bf16[128,1536]{1,0:T(8,128)(2,1)S(1)} %slice.175), channel_id=1, source_target_pairs={{0,2},{1,3},{2,0},{3,1},{4,6},{5,7},{6,4},{7,5},{8,10},{9,11},{10,... | collective-permute-start | bytes 1179656 | tf_op jit(solution)/shard_map/ppermute | solution.py:301
  68.2 0.5 collective-permute-done.15
  68.9 1.7 %collective-permute-start.18 = (bf16[64,1536]{1,0:T(8,128)(2,1)S(1)}, bf16[64,1536]{1,0:T(8,128)(2,1)S(1)}, u32[]{:S(2)}, u32[]{:S(2)}) collective-permute-start(bf16[64,1536]{1,0:T(8,128)(2,1)S(1)} %pad_maximum_fusion.3), channel_id=1, source_target_pairs={{0,12},{4,8},{8,4},{12,0},{16,28},{20,24},{24,20},{28,16},{1,13},{... | collective-permute-start | bytes 589832 | tf_op jit(solution)/shard_map/ppermute | solution.py:301
  70.6 0.4 collective-permute-start.19
  71.1 1.4 %collective-permute-start.20 = (bf16[64,1536]{1,0:T(8,128)(2,1)S(1)}, bf16[64,1536]{1,0:T(8,128)(2,1)S(1)}, u32[]{:S(2)}, u32[]{:S(2)}) collective-permute-start(bf16[64,1536]{1,0:T(8,128)(2,1)S(1)} %pad_maximum_fusion.2), channel_id=1, source_target_pairs={{0,4},{4,0},{8,12},{12,8},{16,20},{20,16},{24,28},{28,24},{1,5},{5... | collective-permute-start | bytes 589832 | tf_op jit(solution)/shard_map/ppermute | solution.py:301
  72.5 6.8 %shard_map.98 = (f32[2,3072,1024]{2,1,0:T(8,128)}, f32[2,3072,1024]{2,1,0:T(8,128)}) custom-call(bf16[2,320,3072]{2,1,0:T(8,128)(2,1)S(1)} %copy-done, bf16[2,320,1024]{2,1,0:T(8,128)(2,1)S(1)} %get-tuple-element.78.gate_grad, bf16[2,320,1024]{2,1,0:T(8,128)(2,1)S(1)} %get-tuple-element.79.up_grad), custom_call_target="tpu_custom_call" | custom-call | flops 2684354560 | bytes 16777216 | tf_op jit(solution)/shard_map/pallas_call | solution.py:266
  79.3 1.0 collective-permute-done.19
  80.4 0.9 collective-permute-done.20
  81.4 0.6 collective-permute-start.21
  82.0 1.4 %collective-permute-start.22 = (bf16[32,1536]{1,0:T(8,128)(2,1)S(1)}, bf16[32,1536]{1,0:T(8,128)(2,1)S(1)}, u32[]{:S(2)}, u32[]{:S(2)}) collective-permute-start(bf16[32,1536]{1,0:T(8,128)(2,1)S(1)} %get-tuple-element.97), channel_id=1, source_target_pairs={{0,4},{4,0},{8,12},{12,8},{16,20},{20,16},{24,28},{28,24},{1,5},{5... | collective-permute-start | bytes 294920 | tf_op jit(solution)/shard_map/ppermute | solution.py:301
  83.5 1.5 %collective-permute-start.23 = (bf16[32,1536]{1,0:T(8,128)(2,1)S(1)}, bf16[32,1536]{1,0:T(8,128)(2,1)S(1)}, u32[]{:S(2)}, u32[]{:S(2)}) collective-permute-start(bf16[32,1536]{1,0:T(8,128)(2,1)S(1)} %get-tuple-element.98), channel_id=1, source_target_pairs={{0,12},{4,8},{8,4},{12,0},{16,28},{20,24},{24,20},{28,16},{1,13},{... | collective-permute-start | bytes 294920 | tf_op jit(solution)/shard_map/ppermute | solution.py:301
  85.0 1.1 %collective-permute-start.24 = (bf16[32,1536]{1,0:T(8,128)(2,1)S(1)}, bf16[32,1536]{1,0:T(8,128)(2,1)S(1)}, u32[]{:S(2)}, u32[]{:S(2)}) collective-permute-start(bf16[32,1536]{1,0:T(8,128)(2,1)S(1)} %add_convert_fusion.11), channel_id=1, source_target_pairs={{0,2},{1,3},{2,0},{3,1},{4,6},{5,7},{6,4},{7,5},{8,10},{9,11},{10,... | collective-permute-start | bytes 294920 | tf_op jit(solution)/shard_map/ppermute | solution.py:301
  86.1 2.8 %shard_map.99 = (f32[2,3072,1024]{2,1,0:T(8,128)}, f32[2,3072,1024]{2,1,0:T(8,128)}) custom-call(bf16[2,320,3072]{2,1,0:T(8,128)(2,1)S(1)} %copy-done, bf16[2,320,1024]{2,1,0:T(8,128)(2,1)S(1)} %get-tuple-element.78.gate_grad, bf16[2,320,1024]{2,1,0:T(8,128)(2,1)S(1)} %get-tuple-element.79.up_grad, ...), custom_call_target="tpu_custom_call", output_to_operand_aliasing={{0}: (3, {}), {1}: (4, {})} | custom-call | flops 671088640 | bytes 4194304 | tf_op jit(solution)/shard_map/pallas_call | solution.py:266
  89.0 0.6 collective-permute-done.24
  89.8 2.7 %collective-permute-start.25 = (bf16[32,3072]{1,0:T(8,128)(2,1)S(1)}, bf16[32,3072]{1,0:T(8,128)(2,1)S(1)}, u32[]{:S(2)}, u32[]{:S(2)}) collective-permute-start(bf16[32,3072]{1,0:T(8,128)(2,1)S(1)} %pad_maximum_fusion.4), channel_id=1, source_target_pairs={{0,16},{4,20},{8,24},{12,28},{16,0},{20,4},{24,8},{28,12},{1,17},{... | collective-permute-start | bytes 589832 | tf_op jit(solution)/shard_map/ppermute | solution.py:301
  92.4 6.8 %shard_map.100 = (f32[2,3072,1024]{2,1,0:T(8,128)}, f32[2,3072,1024]{2,1,0:T(8,128)}) custom-call(bf16[2,320,3072]{2,1,0:T(8,128)(2,1)S(1)} %copy-done, bf16[2,320,1024]{2,1,0:T(8,128)(2,1)S(1)} %get-tuple-element.78.gate_grad, bf16[2,320,1024]{2,1,0:T(8,128)(2,1)S(1)} %get-tuple-element.79.up_grad, ...), custom_call_target="tpu_custom_call", output_to_operand_aliasing={{0}: (3, {}), {1}: (4, {})} | custom-call | flops 2684354560 | bytes 16777216 | tf_op jit(solution)/shard_map/pallas_call | solution.py:266
  99.3 0.7 collective-permute-done.25
  100.0 0.8 collective-permute-start.28
  100.8 0.7 collective-permute-start.27
  101.5 2.1 %collective-permute-start.26 = (bf16[32,3072]{1,0:T(8,128)(2,1)S(1)}, bf16[32,3072]{1,0:T(8,128)(2,1)S(1)}, u32[]{:S(2)}, u32[]{:S(2)}) collective-permute-start(bf16[32,3072]{1,0:T(8,128)(2,1)S(1)} %add_convert_fusion.2), channel_id=1, source_target_pairs={{0,8},{4,12},{8,0},{12,4},{16,24},{20,28},{24,16},{28,20},{1,9},{5... | collective-permute-start | bytes 589832 | tf_op jit(solution)/shard_map/ppermute | solution.py:301
  103.6 5.5 %shard_map.101 = (f32[2,3072,1024]{2,1,0:T(8,128)}, f32[2,3072,1024]{2,1,0:T(8,128)}) custom-call(bf16[2,320,3072]{2,1,0:T(8,128)(2,1)S(1)} %copy-done, bf16[2,320,1024]{2,1,0:T(8,128)(2,1)S(1)} %get-tuple-element.78.gate_grad, bf16[2,320,1024]{2,1,0:T(8,128)(2,1)S(1)} %get-tuple-element.79.up_grad, ...), custom_call_target="tpu_custom_call", output_to_operand_aliasing={{0}: (3, {}), {1}: (4, {})} | custom-call | flops 2013265920 | bytes 12582912 | tf_op jit(solution)/shard_map/pallas_call | solution.py:266
  109.1 1.8 %collective-permute-done.27 = bf16[32,3072]{1,0:T(8,128)(2,1)S(1)} collective-permute-done((bf16[32,3072]{1,0:T(8,128)(2,1)S(1)}, bf16[32,3072]{1,0:T(8,128)(2,1)S(1)}, u32[]{:S(2)}, u32[]{:S(2)}) %collective-permute-start.27) | collective-permute-done | bytes 196640 | tf_op jit(solution)/shard_map/ppermute | solution.py:301
  111.0 0.4 collective-permute-done.26
  111.6 1.0 reverse_select_fusion
  (63 shorter events, 2.2 us)
Async XLA Ops:
  1.7 12.4 %collective-permute-start = (bf16[128,3072]{1,0:T(8,128)(2,1)}, bf16[128,3072]{1,0:T(8,128)(2,1)S(1)}, u32[]{:S(2)}, u32[]{:S(2)}) collective-permute-start(bf16[128,3072]{1,0:T(8,128)(2,1)} %refs_0_), channel_id=1, source_target_pairs={{0,1},{1,0},{2,3},{3,2},{4,5},{5,4},{6,7},{7,6},{8,9},{9,8},{10,11... | collective-permute-start | bytes 2359304 | tf_op jit(solution)/shard_map/ppermute | solution.py:301
  2.3 8.4 %collective-permute-start.5 = (bf16[32,3072]{1,0:T(8,128)(2,1)S(1)}, bf16[32,3072]{1,0:T(8,128)(2,1)S(1)}, u32[]{:S(2)}, u32[]{:S(2)}) collective-permute-start(bf16[32,3072]{1,0:T(8,128)(2,1)S(1)} %get-tuple-element.71), channel_id=1, source_target_pairs={{0,2},{1,3},{2,0},{3,1},{4,6},{5,7},{6,4},{7,5},{8,10},{9,11},{10,... | collective-permute-start | bytes 589832 | tf_op jit(solution)/shard_map/ppermute | solution.py:301
  4.8 12.5 %collective-permute-start.6 = (bf16[32,3072]{1,0:T(8,128)(2,1)S(1)}, bf16[32,3072]{1,0:T(8,128)(2,1)S(1)}, u32[]{:S(2)}, u32[]{:S(2)}) collective-permute-start(bf16[32,3072]{1,0:T(8,128)(2,1)S(1)} %get-tuple-element.72), channel_id=1, source_target_pairs={{0,2},{1,3},{2,0},{3,1},{4,6},{5,7},{6,4},{7,5},{8,10},{9,11},{10,... | collective-permute-start | bytes 589832 | tf_op jit(solution)/shard_map/ppermute | solution.py:301
  10.6 7.0 %collective-permute-start.8 = (bf16[32,3072]{1,0:T(8,128)(2,1)S(1)}, bf16[32,3072]{1,0:T(8,128)(2,1)S(1)}, u32[]{:S(2)}, u32[]{:S(2)}) collective-permute-start(bf16[32,3072]{1,0:T(8,128)(2,1)S(1)} %collective-permute-done.5.refs_2_), channel_id=1, source_target_pairs={{0,8},{4,12},{8,0},{12,4},{16,24},{20,28},{24,16},{28,20},{1,9},{5... | collective-permute-start | bytes 589832 | tf_op jit(solution)/shard_map/ppermute | solution.py:301
  12.6 6.5 %collective-permute-start.7 = (bf16[32,3072]{1,0:T(8,128)(2,1)S(1)}, bf16[32,3072]{1,0:T(8,128)(2,1)S(1)}, u32[]{:S(2)}, u32[]{:S(2)}) collective-permute-start(bf16[32,3072]{1,0:T(8,128)(2,1)S(1)} %collective-permute-done.5.refs_2_), channel_id=1, source_target_pairs={{0,4},{4,0},{8,12},{12,8},{16,20},{20,16},{24,28},{28,24},{1,5},{5... | collective-permute-start | bytes 589832 | tf_op jit(solution)/shard_map/ppermute | solution.py:301
  14.1 7.9 %copy-start.2 = (bf16[128,3072]{1,0:T(8,128)(2,1)}, bf16[128,3072]{1,0:T(8,128)(2,1)S(1)}, u32[]{:S(2)}) copy-start(bf16[128,3072]{1,0:T(8,128)(2,1)S(1)} %collective-permute-done.refs_1_) | copy-start | bytes 2359300
  15.6 3.5 %collective-permute-start.1 = (f32[2,2,128]{2,0,1:T(2,128)S(1)}, f32[2,2,128]{2,0,1:T(2,128)S(1)}, u32[]{:S(2)}, u32[]{:S(2)}) collective-permute-start(f32[2,2,128]{2,0,1:T(2,128)S(1)} %get-tuple-element.147), channel_id=1, source_target_pairs={{0,1},{1,0},{2,3},{3,2},{4,5},{5,4},{6,7},{7,6},{8,9},{9,8},{10,11... | collective-permute-start | bytes 6152 | tf_op jit(solution)/shard_map/ppermute | solution.py:301
  15.7 3.9 %collective-permute-start.2 = (f32[2,2,128]{2,0,1:T(2,128)S(1)}, f32[2,2,128]{2,0,1:T(2,128)S(1)}, u32[]{:S(2)}, u32[]{:S(2)}) collective-permute-start(f32[2,2,128]{2,0,1:T(2,128)S(1)} %get-tuple-element.148), channel_id=1, source_target_pairs={{0,2},{1,3},{2,0},{3,1},{4,6},{5,7},{6,4},{7,5},{8,10},{9,11},{10,... | collective-permute-start | bytes 6152 | tf_op jit(solution)/shard_map/ppermute | solution.py:301
  17.3 3.0 %collective-permute-start.3 = (f32[2,2,128]{2,0,1:T(2,128)S(1)}, f32[2,2,128]{2,0,1:T(2,128)S(1)}, u32[]{:S(2)}, u32[]{:S(2)}) collective-permute-start(f32[2,2,128]{2,0,1:T(2,128)S(1)} %get-tuple-element.149), channel_id=1, source_target_pairs={{0,3},{1,2},{2,1},{3,0},{4,7},{5,6},{6,5},{7,4},{8,11},{9,10},{10,... | collective-permute-start | bytes 6152 | tf_op jit(solution)/shard_map/ppermute | solution.py:301
  17.6 20.3 %collective-permute-start.13 = (bf16[128,3072]{1,0:T(8,128)(2,1)}, bf16[128,3072]{1,0:T(8,128)(2,1)S(1)}, u32[]{:S(2)}, u32[]{:S(2)}) collective-permute-start(bf16[128,3072]{1,0:T(8,128)(2,1)} %refs_0_.1), channel_id=1, source_target_pairs={{0,2},{1,3},{2,0},{3,1},{4,6},{5,7},{6,4},{7,5},{8,10},{9,11},{10,... | collective-permute-start | bytes 2359304 | tf_op jit(solution)/shard_map/ppermute | solution.py:301
  19.1 2.4 %collective-permute-start.9 = (bf16[32,3072]{1,0:T(8,128)(2,1)S(1)}, bf16[32,3072]{1,0:T(8,128)(2,1)S(1)}, u32[]{:S(2)}, u32[]{:S(2)}) collective-permute-start(bf16[32,3072]{1,0:T(8,128)(2,1)S(1)} %collective-permute-done.5.refs_2_), channel_id=1, source_target_pairs={{0,1},{1,0},{2,3},{3,2},{4,5},{5,4},{6,7},{7,6},{8,9},{9,8},{10,11... | collective-permute-start | bytes 589832 | tf_op jit(solution)/shard_map/ppermute | solution.py:301
  19.2 2.8 %collective-permute-start.10 = (bf16[32,3072]{1,0:T(8,128)(2,1)S(1)}, bf16[32,3072]{1,0:T(8,128)(2,1)S(1)}, u32[]{:S(2)}, u32[]{:S(2)}) collective-permute-start(bf16[32,3072]{1,0:T(8,128)(2,1)S(1)} %collective-permute-done.6.refs_3_), channel_id=1, source_target_pairs={{0,1},{1,0},{2,3},{3,2},{4,5},{5,4},{6,7},{7,6},{8,9},{9,8},{10,11... | collective-permute-start | bytes 589832 | tf_op jit(solution)/shard_map/ppermute | solution.py:301
  19.6 2.3 %collective-permute-start.12 = (bf16[32,3072]{1,0:T(8,128)(2,1)S(1)}, bf16[32,3072]{1,0:T(8,128)(2,1)S(1)}, u32[]{:S(2)}, u32[]{:S(2)}) collective-permute-start(bf16[32,3072]{1,0:T(8,128)(2,1)S(1)} %collective-permute-done.8.refs_5_), channel_id=1, source_target_pairs={{0,1},{1,0},{2,3},{3,2},{4,5},{5,4},{6,7},{7,6},{8,9},{9,8},{10,11... | collective-permute-start | bytes 589832 | tf_op jit(solution)/shard_map/ppermute | solution.py:301
  20.3 1.6 %collective-permute-start.11 = (bf16[32,3072]{1,0:T(8,128)(2,1)S(1)}, bf16[32,3072]{1,0:T(8,128)(2,1)S(1)}, u32[]{:S(2)}, u32[]{:S(2)}) collective-permute-start(bf16[32,3072]{1,0:T(8,128)(2,1)S(1)} %collective-permute-done.7.refs_4_), channel_id=1, source_target_pairs={{0,1},{1,0},{2,3},{3,2},{4,5},{5,4},{6,7},{7,6},{8,9},{9,8},{10,11... | collective-permute-start | bytes 589832 | tf_op jit(solution)/shard_map/ppermute | solution.py:301
  21.5 18.7 %copy-start.1 = (bf16[128,3072]{1,0:T(8,128)(2,1)S(1)}, bf16[128,3072]{1,0:T(8,128)(2,1)}, u32[]{:S(2)}) copy-start(bf16[128,3072]{1,0:T(8,128)(2,1)} %refs_0_.1) | copy-start | bytes 2359300
  21.5 16.6 %collective-permute-start.4 = (bf16[128,3072]{1,0:T(8,128)(2,1)}, bf16[128,3072]{1,0:T(8,128)(2,1)S(1)}, u32[]{:S(2)}, u32[]{:S(2)}) collective-permute-start(bf16[128,3072]{1,0:T(8,128)(2,1)} %refs_0_.1), channel_id=1, source_target_pairs={{0,1},{1,0},{2,3},{3,2},{4,5},{5,4},{6,7},{7,6},{8,9},{9,8},{10,11... | collective-permute-start | bytes 2359304 | tf_op jit(solution)/shard_map/ppermute | solution.py:301
  37.9 2.4 %collective-permute-start.14 = (bf16[128,3072]{1,0:T(8,128)(2,1)S(1)}, bf16[128,3072]{1,0:T(8,128)(2,1)S(1)}, u32[]{:S(2)}, u32[]{:S(2)}) collective-permute-start(bf16[128,3072]{1,0:T(8,128)(2,1)S(1)} %collective-permute-done.13.refs_2_), channel_id=1, source_target_pairs={{0,1},{1,0},{2,3},{3,2},{4,5},{5,4},{6,7},{7,6},{8,9},{9,8},{10,11... | collective-permute-start | bytes 2359304 | tf_op jit(solution)/shard_map/ppermute | solution.py:301
  58.0 8.8 %collective-permute-start.16 = (bf16[256,1536]{1,0:T(8,128)(2,1)S(1)}, bf16[256,1536]{1,0:T(8,128)(2,1)S(1)}, u32[]{:S(2)}, u32[]{:S(2)}) collective-permute-start(bf16[256,1536]{1,0:T(8,128)(2,1)S(1)} %get-tuple-element.83), channel_id=1, source_target_pairs={{0,1},{1,0},{2,3},{3,2},{4,5},{5,4},{6,7},{7,6},{8,9},{9,8},{10,11... | collective-permute-start | bytes 2359304 | tf_op jit(solution)/shard_map/ppermute | solution.py:301
  66.4 2.4 %collective-permute-start.15 = (bf16[256,1536]{1,0:T(8,128)(2,1)S(1)}, bf16[256,1536]{1,0:T(8,128)(2,1)S(1)}, u32[]{:S(2)}, u32[]{:S(2)}) collective-permute-start(bf16[256,1536]{1,0:T(8,128)(2,1)S(1)} %get-tuple-element.81), channel_id=1, source_target_pairs={{0,1},{1,0},{2,3},{3,2},{4,5},{5,4},{6,7},{7,6},{8,9},{9,8},{10,11... | collective-permute-start | bytes 2359304 | tf_op jit(solution)/shard_map/ppermute | solution.py:301
  66.8 5.7 %copy-start = (bf16[2,320,3072]{2,1,0:T(8,128)(2,1)S(1)}, bf16[2,320,3072]{2,1,0:T(8,128)(2,1)}, u32[]{:S(2)}) copy-start(bf16[2,320,3072]{2,1,0:T(8,128)(2,1)} %get-tuple-element.117.rows) | copy-start | bytes 11796484
  67.0 14.3 %collective-permute-start.17 = (bf16[128,1536]{1,0:T(8,128)(2,1)S(1)}, bf16[128,1536]{1,0:T(8,128)(2,1)S(1)}, u32[]{:S(2)}, u32[]{:S(2)}) collective-permute-start(bf16[128,1536]{1,0:T(8,128)(2,1)S(1)} %slice.175), channel_id=1, source_target_pairs={{0,2},{1,3},{2,0},{3,1},{4,6},{5,7},{6,4},{7,5},{8,10},{9,11},{10,... | collective-permute-start | bytes 1179656 | tf_op jit(solution)/shard_map/ppermute | solution.py:301
  68.9 10.4 %collective-permute-start.18 = (bf16[64,1536]{1,0:T(8,128)(2,1)S(1)}, bf16[64,1536]{1,0:T(8,128)(2,1)S(1)}, u32[]{:S(2)}, u32[]{:S(2)}) collective-permute-start(bf16[64,1536]{1,0:T(8,128)(2,1)S(1)} %pad_maximum_fusion.3), channel_id=1, source_target_pairs={{0,12},{4,8},{8,4},{12,0},{16,28},{20,24},{24,20},{28,16},{1,13},{... | collective-permute-start | bytes 589832 | tf_op jit(solution)/shard_map/ppermute | solution.py:301
  70.6 9.8 %collective-permute-start.19 = (bf16[64,1536]{1,0:T(8,128)(2,1)S(1)}, bf16[64,1536]{1,0:T(8,128)(2,1)S(1)}, u32[]{:S(2)}, u32[]{:S(2)}) collective-permute-start(bf16[64,1536]{1,0:T(8,128)(2,1)S(1)} %pad_maximum_fusion.1), channel_id=1, source_target_pairs={{0,8},{4,12},{8,0},{12,4},{16,24},{20,28},{24,16},{28,20},{1,9},{5... | collective-permute-start | bytes 589832 | tf_op jit(solution)/shard_map/ppermute | solution.py:301
  71.1 10.2 %collective-permute-start.20 = (bf16[64,1536]{1,0:T(8,128)(2,1)S(1)}, bf16[64,1536]{1,0:T(8,128)(2,1)S(1)}, u32[]{:S(2)}, u32[]{:S(2)}) collective-permute-start(bf16[64,1536]{1,0:T(8,128)(2,1)S(1)} %pad_maximum_fusion.2), channel_id=1, source_target_pairs={{0,4},{4,0},{8,12},{12,8},{16,20},{20,16},{24,28},{28,24},{1,5},{5... | collective-permute-start | bytes 589832 | tf_op jit(solution)/shard_map/ppermute | solution.py:301
  81.4 7.5 %collective-permute-start.21 = (bf16[32,1536]{1,0:T(8,128)(2,1)S(1)}, bf16[32,1536]{1,0:T(8,128)(2,1)S(1)}, u32[]{:S(2)}, u32[]{:S(2)}) collective-permute-start(bf16[32,1536]{1,0:T(8,128)(2,1)S(1)} %get-tuple-element.96), channel_id=1, source_target_pairs={{0,8},{4,12},{8,0},{12,4},{16,24},{20,28},{24,16},{28,20},{1,9},{5... | collective-permute-start | bytes 294920 | tf_op jit(solution)/shard_map/ppermute | solution.py:301
  82.0 6.8 %collective-permute-start.22 = (bf16[32,1536]{1,0:T(8,128)(2,1)S(1)}, bf16[32,1536]{1,0:T(8,128)(2,1)S(1)}, u32[]{:S(2)}, u32[]{:S(2)}) collective-permute-start(bf16[32,1536]{1,0:T(8,128)(2,1)S(1)} %get-tuple-element.97), channel_id=1, source_target_pairs={{0,4},{4,0},{8,12},{12,8},{16,20},{20,16},{24,28},{28,24},{1,5},{5... | collective-permute-start | bytes 294920 | tf_op jit(solution)/shard_map/ppermute | solution.py:301
  83.5 5.5 %collective-permute-start.23 = (bf16[32,1536]{1,0:T(8,128)(2,1)S(1)}, bf16[32,1536]{1,0:T(8,128)(2,1)S(1)}, u32[]{:S(2)}, u32[]{:S(2)}) collective-permute-start(bf16[32,1536]{1,0:T(8,128)(2,1)S(1)} %get-tuple-element.98), channel_id=1, source_target_pairs={{0,12},{4,8},{8,4},{12,0},{16,28},{20,24},{24,20},{28,16},{1,13},{... | collective-permute-start | bytes 294920 | tf_op jit(solution)/shard_map/ppermute | solution.py:301
  85.0 4.6 %collective-permute-start.24 = (bf16[32,1536]{1,0:T(8,128)(2,1)S(1)}, bf16[32,1536]{1,0:T(8,128)(2,1)S(1)}, u32[]{:S(2)}, u32[]{:S(2)}) collective-permute-start(bf16[32,1536]{1,0:T(8,128)(2,1)S(1)} %add_convert_fusion.11), channel_id=1, source_target_pairs={{0,2},{1,3},{2,0},{3,1},{4,6},{5,7},{6,4},{7,5},{8,10},{9,11},{10,... | collective-permute-start | bytes 294920 | tf_op jit(solution)/shard_map/ppermute | solution.py:301
  89.8 10.2 %collective-permute-start.25 = (bf16[32,3072]{1,0:T(8,128)(2,1)S(1)}, bf16[32,3072]{1,0:T(8,128)(2,1)S(1)}, u32[]{:S(2)}, u32[]{:S(2)}) collective-permute-start(bf16[32,3072]{1,0:T(8,128)(2,1)S(1)} %pad_maximum_fusion.4), channel_id=1, source_target_pairs={{0,16},{4,20},{8,24},{12,28},{16,0},{20,4},{24,8},{28,12},{1,17},{... | collective-permute-start | bytes 589832 | tf_op jit(solution)/shard_map/ppermute | solution.py:301
  100.0 9.1 %collective-permute-start.28 = (bf16[32,3072]{1,0:T(8,128)(2,1)S(1)}, bf16[32,3072]{1,0:T(8,128)(2,1)S(1)}, u32[]{:S(2)}, u32[]{:S(2)}) collective-permute-start(bf16[32,3072]{1,0:T(8,128)(2,1)S(1)} %add_convert_fusion.2), channel_id=1, source_target_pairs={{0,12},{4,8},{8,4},{12,0},{16,28},{20,24},{24,20},{28,16},{1,13},{... | collective-permute-start | bytes 589832 | tf_op jit(solution)/shard_map/ppermute | solution.py:301
  100.8 10.1 %collective-permute-start.27 = (bf16[32,3072]{1,0:T(8,128)(2,1)S(1)}, bf16[32,3072]{1,0:T(8,128)(2,1)S(1)}, u32[]{:S(2)}, u32[]{:S(2)}) collective-permute-start(bf16[32,3072]{1,0:T(8,128)(2,1)S(1)} %add_convert_fusion.2), channel_id=1, source_target_pairs={{0,4},{4,0},{8,12},{12,8},{16,20},{20,16},{24,28},{28,24},{1,5},{5... | collective-permute-start | bytes 589832 | tf_op jit(solution)/shard_map/ppermute | solution.py:301
  101.5 9.8 %collective-permute-start.26 = (bf16[32,3072]{1,0:T(8,128)(2,1)S(1)}, bf16[32,3072]{1,0:T(8,128)(2,1)S(1)}, u32[]{:S(2)}, u32[]{:S(2)}) collective-permute-start(bf16[32,3072]{1,0:T(8,128)(2,1)S(1)} %add_convert_fusion.2), channel_id=1, source_target_pairs={{0,8},{4,12},{8,0},{12,4},{16,24},{20,28},{24,16},{28,20},{1,9},{5... | collective-permute-start | bytes 589832 | tf_op jit(solution)/shard_map/ppermute | solution.py:301

commit v2 on v1

--- a/solution.py
+++ b/solution.py
@@ -343,7 +343,9 @@
     for r in range(4):
         part = lax.dynamic_slice_in_dim(table, (me ^ r) * experts, experts, 0)
         tables.append(flip(part, "expert", r) if r > 0 else part)
+    x_across, tables[1] = lax.optimization_barrier((x_across, tables[1]))
     x_far = (x_across, x_corner, flip(x_across, "dp", 1), flip(x_across, "dp", 2))
+    x_far = lax.optimization_barrier(x_far)
     g_across = flip(out_grad, "expert", 2)
     x_far = (*x_far, *to_core(x_far))
     table = jnp.stack(tables, axis=2)

time: 113 us -> 113 us (level)
  starting transfers between devices: 27.9 us -> 29.7 us
  waiting for transfers between devices: 14.5 us -> 13 us
    ppermute x29, starting transfers between devices: 27.9 us -> 29.7 us  [flip(): return lax.ppermute(value, axis, [(i, i ^ bit) for i in range(count)])]
    ppermute x29, waiting for transfers between devices: 14.5 us -> 13 us  [flip(): return lax.ppermute(value, axis, [(i, i ^ bit) for i in range(count)])]
  transfers between devices with their start and end apart: 29 -> 29, of which waited for: 11 -> 14; matrix products, arithmetic and copies ran while one was open for 3% -> 3% of each run, Pallas kernels for 41% -> 41%
where the time goes in v2:
time: 113 us
  Pallas kernels  63.7 us (56%)
  starting transfers between devices  29.7 us (26%)
  waiting for transfers between devices  13 us (12%)
  other arithmetic  3.85 us (3%)
  local copies, waits for them, and re-layouts  1.54 us (1%)
    ppermute x29, starting transfers between devices, flip(): return lax.ppermute(value, axis, [(i, i ^ bit) for i in range(count)])  29.7 us
    pallas_call x4, Pallas kernels, weight_grads(): pl.pallas_call(weights_kernel, grid=(steps,), in_specs=[pl.BlockSpec((1,...  21.9 us
    pallas_call x2, Pallas kernels, input_sums(): pl.pallas_call(functools.partial(inputs_kernel, groups), grid=(steps,), i...  16.2 us
    pallas_call x1, Pallas kernels, forward(): pl.pallas_call(functools.partial(forward_kernel, len(pieces)), grid=(expe...  15.9 us
    ppermute x29, waiting for transfers between devices, flip(): return lax.ppermute(value, axis, [(i, i ^ bit) for i in range(count)])  13 us
    pallas_call x1, Pallas kernels, hidden_grads(): pl.pallas_call(functools.partial(hidden_kernel, len(pieces)), grid=(exper...  9.63 us
  transfers between devices with their start and end apart: 29, of which 14 were waited for; matrix products, arithmetic and copies ran while one was open for 3% of the time, Pallas kernels for 41%

profile of v2, /device:TPU:0, one launch (start us, length us, event | category | flops | bytes accessed | tf_op | source)
XLA Modules:
  0.0 112.8 jit_solution(12934954276618740368)
XLA Ops:
  0.7 1.1 constant_dynamic-slice_fusion
  1.7 0.5 collective-permute-start
  2.3 2.6 %collective-permute-start.1 = (bf16[32,3072]{1,0:T(8,128)(2,1)S(1)}, bf16[32,3072]{1,0:T(8,128)(2,1)S(1)}, u32[]{:S(2)}, u32[]{:S(2)}) collective-permute-start(bf16[32,3072]{1,0:T(8,128)(2,1)S(1)} %get-tuple-element.74), channel_id=1, source_target_pairs={{0,2},{1,3},{2,0},{3,1},{4,6},{5,7},{6,4},{7,5},{8,10},{9,11},{10,... | collective-permute-start | bytes 589832 | tf_op jit(solution)/shard_map/ppermute | solution.py:301
  4.9 0.7 fusion.1
  5.7 0.7 select_reduce_fusion
  6.6 2.4 %collective-permute-start.3 = (f32[2,2,128]{2,0,1:T(2,128)S(1)}, f32[2,2,128]{2,0,1:T(2,128)S(1)}, u32[]{:S(2)}, u32[]{:S(2)}) collective-permute-start(f32[2,2,128]{2,0,1:T(2,128)S(1)} %get-tuple-element.160), channel_id=1, source_target_pairs={{0,2},{1,3},{2,0},{3,1},{4,6},{5,7},{6,4},{7,5},{8,10},{9,11},{10,... | collective-permute-start | bytes 6152 | tf_op jit(solution)/shard_map/ppermute | solution.py:301
  9.0 1.7 %collective-permute-start.6 = (bf16[32,3072]{1,0:T(8,128)(2,1)S(1)}, bf16[32,3072]{1,0:T(8,128)(2,1)S(1)}, u32[]{:S(2)}, u32[]{:S(2)}) collective-permute-start(bf16[32,3072]{1,0:T(8,128)(2,1)S(1)} %get-tuple-element.80), channel_id=1, source_target_pairs={{0,2},{1,3},{2,0},{3,1},{4,6},{5,7},{6,4},{7,5},{8,10},{9,11},{10,... | collective-permute-start | bytes 589832 | tf_op jit(solution)/shard_map/ppermute | solution.py:301
  10.7 1.4 %collective-permute-start.13 = (bf16[128,3072]{1,0:T(8,128)(2,1)}, bf16[128,3072]{1,0:T(8,128)(2,1)S(1)}, u32[]{:S(2)}, u32[]{:S(2)}) collective-permute-start(bf16[128,3072]{1,0:T(8,128)(2,1)} %refs_0_.1), channel_id=1, source_target_pairs={{0,2},{1,3},{2,0},{3,1},{4,6},{5,7},{6,4},{7,5},{8,10},{9,11},{10,... | collective-permute-start | bytes 2359304 | tf_op jit(solution)/shard_map/ppermute | solution.py:301
  12.1 1.6 %collective-permute-start.8 = (bf16[32,3072]{1,0:T(8,128)(2,1)S(1)}, bf16[32,3072]{1,0:T(8,128)(2,1)S(1)}, u32[]{:S(2)}, u32[]{:S(2)}) collective-permute-start(bf16[32,3072]{1,0:T(8,128)(2,1)S(1)} %collective-permute-done.1.refs_2_), channel_id=1, source_target_pairs={{0,8},{4,12},{8,0},{12,4},{16,24},{20,28},{24,16},{28,20},{1,9},{5... | collective-permute-start | bytes 589832 | tf_op jit(solution)/shard_map/ppermute | solution.py:301
  13.7 1.5 %collective-permute-start.7 = (bf16[32,3072]{1,0:T(8,128)(2,1)S(1)}, bf16[32,3072]{1,0:T(8,128)(2,1)S(1)}, u32[]{:S(2)}, u32[]{:S(2)}) collective-permute-start(bf16[32,3072]{1,0:T(8,128)(2,1)S(1)} %collective-permute-done.1.refs_2_), channel_id=1, source_target_pairs={{0,4},{4,0},{8,12},{12,8},{16,20},{20,16},{24,28},{28,24},{1,5},{5... | collective-permute-start | bytes 589832 | tf_op jit(solution)/shard_map/ppermute | solution.py:301
  16.0 0.8 collective-permute-done.6.refs_3_
  16.8 1.5 %collective-permute-done.8.refs_5_ = bf16[32,3072]{1,0:T(8,128)(2,1)S(1)} collective-permute-done((bf16[32,3072]{1,0:T(8,128)(2,1)S(1)}, bf16[32,3072]{1,0:T(8,128)(2,1)S(1)}, u32[]{:S(2)}, u32[]{:S(2)}) %collective-permute-start.8) | collective-permute-done | bytes 196640 | tf_op jit(solution)/shard_map/ppermute | solution.py:301
  18.3 1.3 %collective-permute-done.7.refs_4_ = bf16[32,3072]{1,0:T(8,128)(2,1)S(1)} collective-permute-done((bf16[32,3072]{1,0:T(8,128)(2,1)S(1)}, bf16[32,3072]{1,0:T(8,128)(2,1)S(1)}, u32[]{:S(2)}, u32[]{:S(2)}) %collective-permute-start.7) | collective-permute-done | bytes 196640 | tf_op jit(solution)/shard_map/ppermute | solution.py:301
  19.6 0.5 collective-permute-start.10
  20.1 0.5 collective-permute-start.12
  21.3 0.3 collective-permute-done.11.refs_8_
  21.6 0.3 collective-permute-done.12.refs_9_
  21.9 15.9 %shard_map.94 = (bf16[2,320,3072]{2,1,0:T(8,128)(2,1)}, f32[2,320,1024]{2,1,0:T(8,128)}, f32[2,320,1024]{2,1,0:T(8,128)}) custom-call(bf16[128,3072]{1,0:T(8,128)(2,1)} %refs_0_, bf16[128,3072]{1,0:T(8,128)(2,1)} %copy-done.2, bf16[32,3072]{1,0:T(8,128)(2,1)S(1)} %collective-permute-done.1.refs_2_, bf16[32,3072]{1,0:T(8,128)(2,1)S(1)} %collective-permute-done.6.refs_3_, ...), custom_call_target="tpu_custom_call" | custom-call | flops 8053063680 | bytes 25165824 | tf_op jit(solution)/shard_map/pallas_call | solution.py:143
  37.8 0.3 collective-permute-start.14
  38.1 2.1 %collective-permute-done.14.refs_3_ = bf16[128,3072]{1,0:T(8,128)(2,1)S(1)} collective-permute-done((bf16[128,3072]{1,0:T(8,128)(2,1)S(1)}, bf16[128,3072]{1,0:T(8,128)(2,1)S(1)}, u32[]{:S(2)}, u32[]{:S(2)}) %collective-permute-start.14) | collective-permute-done | bytes 786464 | tf_op jit(solution)/shard_map/ppermute | solution.py:301
  40.1 9.6 %shard_map.95 = (bf16[2,320,1024]{2,1,0:T(8,128)(2,1)S(1)}, bf16[2,320,1024]{2,1,0:T(8,128)(2,1)S(1)}) custom-call(bf16[128,3072]{1,0:T(8,128)(2,1)S(1)} %copy-done.1, bf16[128,3072]{1,0:T(8,128)(2,1)S(1)} %collective-permute-done.5.refs_1_, bf16[128,3072]{1,0:T(8,128)(2,1)S(1)} %collective-permute-done.13.refs_2_, ...), custom_call_target="tpu_custom_call" | custom-call | flops 4026531840 | bytes 12582912 | tf_op jit(solution)/shard_map/pallas_call | solution.py:190
  49.8 8.1 %shard_map.97 = (bf16[256,1536]{1,0:T(8,128)(2,1)S(1)}, bf16[256,1536]{1,0:T(8,128)(2,1)S(1)}) custom-call(bf16[4,128,160]{2,1,0:T(8,128)(2,1)S(1)} %add_convert_fusion.1.back, bf16[2,320,1024]{2,1,0:T(8,128)(2,1)S(1)} %get-tuple-element.90.gate_grad, bf16[2,320,1024]{2,1,0:T(8,128)(2,1)S(1)} %get-tuple-element.91.up_grad, bf16[2,3072,1024]{2,1,0:T(8,128)(2,1)} %w_gate.3, ...), custom_call_target="tpu_custom_call" | custom-call | flops 4026531840 | bytes 12582912 | tf_op jit(solution)/shard_map/pallas_call | solution.py:227
  57.9 0.3 collective-permute-start.16
  58.2 8.1 %shard_map.96 = (bf16[256,1536]{1,0:T(8,128)(2,1)S(1)}, bf16[256,1536]{1,0:T(8,128)(2,1)S(1)}) custom-call(bf16[4,128,160]{2,1,0:T(8,128)(2,1)S(1)} %add_convert_fusion.1.back, bf16[2,320,1024]{2,1,0:T(8,128)(2,1)S(1)} %get-tuple-element.90.gate_grad, bf16[2,320,1024]{2,1,0:T(8,128)(2,1)S(1)} %get-tuple-element.91.up_grad, bf16[2,3072,1024]{2,1,0:T(8,128)(2,1)} %w_gate.3, ...), custom_call_target="tpu_custom_call" | custom-call | flops 4026531840 | bytes 12582912 | tf_op jit(solution)/shard_map/pallas_call | solution.py:227
  66.3 0.3 collective-permute-start.15
  66.9 1.2 %collective-permute-start.17 = (bf16[128,1536]{1,0:T(8,128)(2,1)S(1)}, bf16[128,1536]{1,0:T(8,128)(2,1)S(1)}, u32[]{:S(2)}, u32[]{:S(2)}) collective-permute-start(bf16[128,1536]{1,0:T(8,128)(2,1)S(1)} %slice.175), channel_id=1, source_target_pairs={{0,2},{1,3},{2,0},{3,1},{4,6},{5,7},{6,4},{7,5},{8,10},{9,11},{10,... | collective-permute-start | bytes 1179656 | tf_op jit(solution)/shard_map/ppermute | solution.py:301
  68.1 0.5 collective-permute-done.15
  68.9 1.4 %collective-permute-start.18 = (bf16[64,1536]{1,0:T(8,128)(2,1)S(1)}, bf16[64,1536]{1,0:T(8,128)(2,1)S(1)}, u32[]{:S(2)}, u32[]{:S(2)}) collective-permute-start(bf16[64,1536]{1,0:T(8,128)(2,1)S(1)} %pad_maximum_fusion.3), channel_id=1, source_target_pairs={{0,12},{4,8},{8,4},{12,0},{16,28},{20,24},{24,20},{28,16},{1,13},{... | collective-permute-start | bytes 589832 | tf_op jit(solution)/shard_map/ppermute | solution.py:301
  70.3 1.6 %collective-permute-start.19 = (bf16[64,1536]{1,0:T(8,128)(2,1)S(1)}, bf16[64,1536]{1,0:T(8,128)(2,1)S(1)}, u32[]{:S(2)}, u32[]{:S(2)}) collective-permute-start(bf16[64,1536]{1,0:T(8,128)(2,1)S(1)} %pad_maximum_fusion.1), channel_id=1, source_target_pairs={{0,8},{4,12},{8,0},{12,4},{16,24},{20,28},{24,16},{28,20},{1,9},{5... | collective-permute-start | bytes 589832 | tf_op jit(solution)/shard_map/ppermute | solution.py:301
  71.9 0.5 collective-permute-start.20
  72.4 6.8 %shard_map.98 = (f32[2,3072,1024]{2,1,0:T(8,128)}, f32[2,3072,1024]{2,1,0:T(8,128)}) custom-call(bf16[2,320,3072]{2,1,0:T(8,128)(2,1)S(1)} %copy-done, bf16[2,320,1024]{2,1,0:T(8,128)(2,1)S(1)} %get-tuple-element.90.gate_grad, bf16[2,320,1024]{2,1,0:T(8,128)(2,1)S(1)} %get-tuple-element.91.up_grad), custom_call_target="tpu_custom_call" | custom-call | flops 2684354560 | bytes 16777216 | tf_op jit(solution)/shard_map/pallas_call | solution.py:266
  79.3 1.9 %collective-permute-done.19 = bf16[64,1536]{1,0:T(8,128)(2,1)S(1)} collective-permute-done((bf16[64,1536]{1,0:T(8,128)(2,1)S(1)}, bf16[64,1536]{1,0:T(8,128)(2,1)S(1)}, u32[]{:S(2)}, u32[]{:S(2)}) %collective-permute-start.19) | collective-permute-done | bytes 196640 | tf_op jit(solution)/shard_map/ppermute | solution.py:301
  81.4 0.5 collective-permute-start.21
  81.9 1.4 %collective-permute-start.22 = (bf16[32,1536]{1,0:T(8,128)(2,1)S(1)}, bf16[32,1536]{1,0:T(8,128)(2,1)S(1)}, u32[]{:S(2)}, u32[]{:S(2)}) collective-permute-start(bf16[32,1536]{1,0:T(8,128)(2,1)S(1)} %get-tuple-element.109), channel_id=1, source_target_pairs={{0,4},{4,0},{8,12},{12,8},{16,20},{20,16},{24,28},{28,24},{1,5},{5... | collective-permute-start | bytes 294920 | tf_op jit(solution)/shard_map/ppermute | solution.py:301
  83.3 1.6 %collective-permute-start.23 = (bf16[32,1536]{1,0:T(8,128)(2,1)S(1)}, bf16[32,1536]{1,0:T(8,128)(2,1)S(1)}, u32[]{:S(2)}, u32[]{:S(2)}) collective-permute-start(bf16[32,1536]{1,0:T(8,128)(2,1)S(1)} %get-tuple-element.110), channel_id=1, source_target_pairs={{0,12},{4,8},{8,4},{12,0},{16,28},{20,24},{24,20},{28,16},{1,13},{... | collective-permute-start | bytes 294920 | tf_op jit(solution)/shard_map/ppermute | solution.py:301
  84.9 1.2 %collective-permute-start.24 = (bf16[32,1536]{1,0:T(8,128)(2,1)S(1)}, bf16[32,1536]{1,0:T(8,128)(2,1)S(1)}, u32[]{:S(2)}, u32[]{:S(2)}) collective-permute-start(bf16[32,1536]{1,0:T(8,128)(2,1)S(1)} %add_convert_fusion.11), channel_id=1, source_target_pairs={{0,2},{1,3},{2,0},{3,1},{4,6},{5,7},{6,4},{7,5},{8,10},{9,11},{10,... | collective-permute-start | bytes 294920 | tf_op jit(solution)/shard_map/ppermute | solution.py:301
  86.1 2.8 %shard_map.99 = (f32[2,3072,1024]{2,1,0:T(8,128)}, f32[2,3072,1024]{2,1,0:T(8,128)}) custom-call(bf16[2,320,3072]{2,1,0:T(8,128)(2,1)S(1)} %copy-done, bf16[2,320,1024]{2,1,0:T(8,128)(2,1)S(1)} %get-tuple-element.90.gate_grad, bf16[2,320,1024]{2,1,0:T(8,128)(2,1)S(1)} %get-tuple-element.91.up_grad, ...), custom_call_target="tpu_custom_call", output_to_operand_aliasing={{0}: (3, {}), {1}: (4, {})} | custom-call | flops 671088640 | bytes 4194304 | tf_op jit(solution)/shard_map/pallas_call | solution.py:266
  88.9 0.2 collective-permute-done.23
  89.1 0.4 collective-permute-done.24
  89.7 2.6 %collective-permute-start.25 = (bf16[32,3072]{1,0:T(8,128)(2,1)S(1)}, bf16[32,3072]{1,0:T(8,128)(2,1)S(1)}, u32[]{:S(2)}, u32[]{:S(2)}) collective-permute-start(bf16[32,3072]{1,0:T(8,128)(2,1)S(1)} %pad_maximum_fusion.4), channel_id=1, source_target_pairs={{0,16},{4,20},{8,24},{12,28},{16,0},{20,4},{24,8},{28,12},{1,17},{... | collective-permute-start | bytes 589832 | tf_op jit(solution)/shard_map/ppermute | solution.py:301
  92.4 6.8 %shard_map.100 = (f32[2,3072,1024]{2,1,0:T(8,128)}, f32[2,3072,1024]{2,1,0:T(8,128)}) custom-call(bf16[2,320,3072]{2,1,0:T(8,128)(2,1)S(1)} %copy-done, bf16[2,320,1024]{2,1,0:T(8,128)(2,1)S(1)} %get-tuple-element.90.gate_grad, bf16[2,320,1024]{2,1,0:T(8,128)(2,1)S(1)} %get-tuple-element.91.up_grad, ...), custom_call_target="tpu_custom_call", output_to_operand_aliasing={{0}: (3, {}), {1}: (4, {})} | custom-call | flops 2684354560 | bytes 16777216 | tf_op jit(solution)/shard_map/pallas_call | solution.py:266
  99.2 1.2 %collective-permute-done.25 = bf16[32,3072]{1,0:T(8,128)(2,1)S(1)} collective-permute-done((bf16[32,3072]{1,0:T(8,128)(2,1)S(1)}, bf16[32,3072]{1,0:T(8,128)(2,1)S(1)}, u32[]{:S(2)}, u32[]{:S(2)}) %collective-permute-start.25) | collective-permute-done | bytes 196640 | tf_op jit(solution)/shard_map/ppermute | solution.py:301
  100.5 0.3 collective-permute-start.28
  100.8 1.0 collective-permute-start.27
  101.8 2.3 %collective-permute-start.26 = (bf16[32,3072]{1,0:T(8,128)(2,1)S(1)}, bf16[32,3072]{1,0:T(8,128)(2,1)S(1)}, u32[]{:S(2)}, u32[]{:S(2)}) collective-permute-start(bf16[32,3072]{1,0:T(8,128)(2,1)S(1)} %add_convert_fusion.2), channel_id=1, source_target_pairs={{0,8},{4,12},{8,0},{12,4},{16,24},{20,28},{24,16},{28,20},{1,9},{5... | collective-permute-start | bytes 589832 | tf_op jit(solution)/shard_map/ppermute | solution.py:301
  104.0 5.5 %shard_map.101 = (f32[2,3072,1024]{2,1,0:T(8,128)}, f32[2,3072,1024]{2,1,0:T(8,128)}) custom-call(bf16[2,320,3072]{2,1,0:T(8,128)(2,1)S(1)} %copy-done, bf16[2,320,1024]{2,1,0:T(8,128)(2,1)S(1)} %get-tuple-element.90.gate_grad, bf16[2,320,1024]{2,1,0:T(8,128)(2,1)S(1)} %get-tuple-element.91.up_grad, ...), custom_call_target="tpu_custom_call", output_to_operand_aliasing={{0}: (3, {}), {1}: (4, {})} | custom-call | flops 2013265920 | bytes 12582912 | tf_op jit(solution)/shard_map/pallas_call | solution.py:266
  109.5 2.0 %collective-permute-done.27 = bf16[32,3072]{1,0:T(8,128)(2,1)S(1)} collective-permute-done((bf16[32,3072]{1,0:T(8,128)(2,1)S(1)}, bf16[32,3072]{1,0:T(8,128)(2,1)S(1)}, u32[]{:S(2)}, u32[]{:S(2)}) %collective-permute-start.27) | collective-permute-done | bytes 196640 | tf_op jit(solution)/shard_map/ppermute | solution.py:301
  111.8 1.0 reverse_select_fusion
  (63 shorter events, 2.8 us)
Async XLA Ops:
  1.7 3.1 %collective-permute-start = (bf16[128,3072]{1,0:T(8,128)(2,1)}, bf16[128,3072]{1,0:T(8,128)(2,1)S(1)}, u32[]{:S(2)}, u32[]{:S(2)}) collective-permute-start(bf16[128,3072]{1,0:T(8,128)(2,1)} %refs_0_), channel_id=1, source_target_pairs={{0,1},{1,0},{2,3},{3,2},{4,5},{5,4},{6,7},{7,6},{8,9},{9,8},{10,11... | collective-permute-start | bytes 2359304 | tf_op jit(solution)/shard_map/ppermute | solution.py:301
  2.3 8.5 %collective-permute-start.1 = (bf16[32,3072]{1,0:T(8,128)(2,1)S(1)}, bf16[32,3072]{1,0:T(8,128)(2,1)S(1)}, u32[]{:S(2)}, u32[]{:S(2)}) collective-permute-start(bf16[32,3072]{1,0:T(8,128)(2,1)S(1)} %get-tuple-element.74), channel_id=1, source_target_pairs={{0,2},{1,3},{2,0},{3,1},{4,6},{5,7},{6,4},{7,5},{8,10},{9,11},{10,... | collective-permute-start | bytes 589832 | tf_op jit(solution)/shard_map/ppermute | solution.py:301
  4.8 17.0 %copy-start.2 = (bf16[128,3072]{1,0:T(8,128)(2,1)}, bf16[128,3072]{1,0:T(8,128)(2,1)S(1)}, u32[]{:S(2)}) copy-start(bf16[128,3072]{1,0:T(8,128)(2,1)S(1)} %collective-permute-done.refs_1_) | copy-start | bytes 2359300
  6.4 5.7 %collective-permute-start.2 = (f32[2,2,128]{2,0,1:T(2,128)S(1)}, f32[2,2,128]{2,0,1:T(2,128)S(1)}, u32[]{:S(2)}, u32[]{:S(2)}) collective-permute-start(f32[2,2,128]{2,0,1:T(2,128)S(1)} %get-tuple-element.159), channel_id=1, source_target_pairs={{0,1},{1,0},{2,3},{3,2},{4,5},{5,4},{6,7},{7,6},{8,9},{9,8},{10,11... | collective-permute-start | bytes 6152 | tf_op jit(solution)/shard_map/ppermute | solution.py:301
  6.6 7.1 %collective-permute-start.3 = (f32[2,2,128]{2,0,1:T(2,128)S(1)}, f32[2,2,128]{2,0,1:T(2,128)S(1)}, u32[]{:S(2)}, u32[]{:S(2)}) collective-permute-start(f32[2,2,128]{2,0,1:T(2,128)S(1)} %get-tuple-element.160), channel_id=1, source_target_pairs={{0,2},{1,3},{2,0},{3,1},{4,6},{5,7},{6,4},{7,5},{8,10},{9,11},{10,... | collective-permute-start | bytes 6152 | tf_op jit(solution)/shard_map/ppermute | solution.py:301
  9.0 6.2 %collective-permute-start.4 = (f32[2,2,128]{2,0,1:T(2,128)S(1)}, f32[2,2,128]{2,0,1:T(2,128)S(1)}, u32[]{:S(2)}, u32[]{:S(2)}) collective-permute-start(f32[2,2,128]{2,0,1:T(2,128)S(1)} %get-tuple-element.161), channel_id=1, source_target_pairs={{0,3},{1,2},{2,1},{3,0},{4,7},{5,6},{6,5},{7,4},{8,11},{9,10},{10,... | collective-permute-start | bytes 6152 | tf_op jit(solution)/shard_map/ppermute | solution.py:301
  9.0 7.7 %collective-permute-start.6 = (bf16[32,3072]{1,0:T(8,128)(2,1)S(1)}, bf16[32,3072]{1,0:T(8,128)(2,1)S(1)}, u32[]{:S(2)}, u32[]{:S(2)}) collective-permute-start(bf16[32,3072]{1,0:T(8,128)(2,1)S(1)} %get-tuple-element.80), channel_id=1, source_target_pairs={{0,2},{1,3},{2,0},{3,1},{4,6},{5,7},{6,4},{7,5},{8,10},{9,11},{10,... | collective-permute-start | bytes 589832 | tf_op jit(solution)/shard_map/ppermute | solution.py:301
  10.7 27.0 %collective-permute-start.13 = (bf16[128,3072]{1,0:T(8,128)(2,1)}, bf16[128,3072]{1,0:T(8,128)(2,1)S(1)}, u32[]{:S(2)}, u32[]{:S(2)}) collective-permute-start(bf16[128,3072]{1,0:T(8,128)(2,1)} %refs_0_.1), channel_id=1, source_target_pairs={{0,2},{1,3},{2,0},{3,1},{4,6},{5,7},{6,4},{7,5},{8,10},{9,11},{10,... | collective-permute-start | bytes 2359304 | tf_op jit(solution)/shard_map/ppermute | solution.py:301
  12.1 6.1 %collective-permute-start.8 = (bf16[32,3072]{1,0:T(8,128)(2,1)S(1)}, bf16[32,3072]{1,0:T(8,128)(2,1)S(1)}, u32[]{:S(2)}, u32[]{:S(2)}) collective-permute-start(bf16[32,3072]{1,0:T(8,128)(2,1)S(1)} %collective-permute-done.1.refs_2_), channel_id=1, source_target_pairs={{0,8},{4,12},{8,0},{12,4},{16,24},{20,28},{24,16},{28,20},{1,9},{5... | collective-permute-start | bytes 589832 | tf_op jit(solution)/shard_map/ppermute | solution.py:301
  13.7 5.9 %collective-permute-start.7 = (bf16[32,3072]{1,0:T(8,128)(2,1)S(1)}, bf16[32,3072]{1,0:T(8,128)(2,1)S(1)}, u32[]{:S(2)}, u32[]{:S(2)}) collective-permute-start(bf16[32,3072]{1,0:T(8,128)(2,1)S(1)} %collective-permute-done.1.refs_2_), channel_id=1, source_target_pairs={{0,4},{4,0},{8,12},{12,8},{16,20},{20,16},{24,28},{28,24},{1,5},{5... | collective-permute-start | bytes 589832 | tf_op jit(solution)/shard_map/ppermute | solution.py:301
  19.6 1.4 %collective-permute-start.9 = (bf16[32,3072]{1,0:T(8,128)(2,1)S(1)}, bf16[32,3072]{1,0:T(8,128)(2,1)S(1)}, u32[]{:S(2)}, u32[]{:S(2)}) collective-permute-start(bf16[32,3072]{1,0:T(8,128)(2,1)S(1)} %collective-permute-done.1.refs_2_), channel_id=1, source_target_pairs={{0,1},{1,0},{2,3},{3,2},{4,5},{5,4},{6,7},{7,6},{8,9},{9,8},{10,11... | collective-permute-start | bytes 589832 | tf_op jit(solution)/shard_map/ppermute | solution.py:301
  19.6 1.7 %collective-permute-start.10 = (bf16[32,3072]{1,0:T(8,128)(2,1)S(1)}, bf16[32,3072]{1,0:T(8,128)(2,1)S(1)}, u32[]{:S(2)}, u32[]{:S(2)}) collective-permute-start(bf16[32,3072]{1,0:T(8,128)(2,1)S(1)} %collective-permute-done.6.refs_3_), channel_id=1, source_target_pairs={{0,1},{1,0},{2,3},{3,2},{4,5},{5,4},{6,7},{7,6},{8,9},{9,8},{10,11... | collective-permute-start | bytes 589832 | tf_op jit(solution)/shard_map/ppermute | solution.py:301
  20.1 1.5 %collective-permute-start.11 = (bf16[32,3072]{1,0:T(8,128)(2,1)S(1)}, bf16[32,3072]{1,0:T(8,128)(2,1)S(1)}, u32[]{:S(2)}, u32[]{:S(2)}) collective-permute-start(bf16[32,3072]{1,0:T(8,128)(2,1)S(1)} %collective-permute-done.7.refs_4_), channel_id=1, source_target_pairs={{0,1},{1,0},{2,3},{3,2},{4,5},{5,4},{6,7},{7,6},{8,9},{9,8},{10,11... | collective-permute-start | bytes 589832 | tf_op jit(solution)/shard_map/ppermute | solution.py:301
  20.1 1.8 %collective-permute-start.12 = (bf16[32,3072]{1,0:T(8,128)(2,1)S(1)}, bf16[32,3072]{1,0:T(8,128)(2,1)S(1)}, u32[]{:S(2)}, u32[]{:S(2)}) collective-permute-start(bf16[32,3072]{1,0:T(8,128)(2,1)S(1)} %collective-permute-done.8.refs_5_), channel_id=1, source_target_pairs={{0,1},{1,0},{2,3},{3,2},{4,5},{5,4},{6,7},{7,6},{8,9},{9,8},{10,11... | collective-permute-start | bytes 589832 | tf_op jit(solution)/shard_map/ppermute | solution.py:301
  20.8 19.3 %copy-start.1 = (bf16[128,3072]{1,0:T(8,128)(2,1)S(1)}, bf16[128,3072]{1,0:T(8,128)(2,1)}, u32[]{:S(2)}) copy-start(bf16[128,3072]{1,0:T(8,128)(2,1)} %refs_0_.1) | copy-start | bytes 2359300
  21.0 17.0 %collective-permute-start.5 = (bf16[128,3072]{1,0:T(8,128)(2,1)}, bf16[128,3072]{1,0:T(8,128)(2,1)S(1)}, u32[]{:S(2)}, u32[]{:S(2)}) collective-permute-start(bf16[128,3072]{1,0:T(8,128)(2,1)} %refs_0_.1), channel_id=1, source_target_pairs={{0,1},{1,0},{2,3},{3,2},{4,5},{5,4},{6,7},{7,6},{8,9},{9,8},{10,11... | collective-permute-start | bytes 2359304 | tf_op jit(solution)/shard_map/ppermute | solution.py:301
  37.8 2.4 %collective-permute-start.14 = (bf16[128,3072]{1,0:T(8,128)(2,1)S(1)}, bf16[128,3072]{1,0:T(8,128)(2,1)S(1)}, u32[]{:S(2)}, u32[]{:S(2)}) collective-permute-start(bf16[128,3072]{1,0:T(8,128)(2,1)S(1)} %collective-permute-done.13.refs_2_), channel_id=1, source_target_pairs={{0,1},{1,0},{2,3},{3,2},{4,5},{5,4},{6,7},{7,6},{8,9},{9,8},{10,11... | collective-permute-start | bytes 2359304 | tf_op jit(solution)/shard_map/ppermute | solution.py:301
  57.9 8.8 %collective-permute-start.16 = (bf16[256,1536]{1,0:T(8,128)(2,1)S(1)}, bf16[256,1536]{1,0:T(8,128)(2,1)S(1)}, u32[]{:S(2)}, u32[]{:S(2)}) collective-permute-start(bf16[256,1536]{1,0:T(8,128)(2,1)S(1)} %get-tuple-element.95), channel_id=1, source_target_pairs={{0,1},{1,0},{2,3},{3,2},{4,5},{5,4},{6,7},{7,6},{8,9},{9,8},{10,11... | collective-permute-start | bytes 2359304 | tf_op jit(solution)/shard_map/ppermute | solution.py:301
  66.3 2.4 %collective-permute-start.15 = (bf16[256,1536]{1,0:T(8,128)(2,1)S(1)}, bf16[256,1536]{1,0:T(8,128)(2,1)S(1)}, u32[]{:S(2)}, u32[]{:S(2)}) collective-permute-start(bf16[256,1536]{1,0:T(8,128)(2,1)S(1)} %get-tuple-element.93), channel_id=1, source_target_pairs={{0,1},{1,0},{2,3},{3,2},{4,5},{5,4},{6,7},{7,6},{8,9},{9,8},{10,11... | collective-permute-start | bytes 2359304 | tf_op jit(solution)/shard_map/ppermute | solution.py:301
  66.7 5.8 %copy-start = (bf16[2,320,3072]{2,1,0:T(8,128)(2,1)S(1)}, bf16[2,320,3072]{2,1,0:T(8,128)(2,1)}, u32[]{:S(2)}) copy-start(bf16[2,320,3072]{2,1,0:T(8,128)(2,1)} %get-tuple-element.129.rows) | copy-start | bytes 11796484
  66.9 14.3 %collective-permute-start.17 = (bf16[128,1536]{1,0:T(8,128)(2,1)S(1)}, bf16[128,1536]{1,0:T(8,128)(2,1)S(1)}, u32[]{:S(2)}, u32[]{:S(2)}) collective-permute-start(bf16[128,1536]{1,0:T(8,128)(2,1)S(1)} %slice.175), channel_id=1, source_target_pairs={{0,2},{1,3},{2,0},{3,1},{4,6},{5,7},{6,4},{7,5},{8,10},{9,11},{10,... | collective-permute-start | bytes 1179656 | tf_op jit(solution)/shard_map/ppermute | solution.py:301
  68.9 10.4 %collective-permute-start.18 = (bf16[64,1536]{1,0:T(8,128)(2,1)S(1)}, bf16[64,1536]{1,0:T(8,128)(2,1)S(1)}, u32[]{:S(2)}, u32[]{:S(2)}) collective-permute-start(bf16[64,1536]{1,0:T(8,128)(2,1)S(1)} %pad_maximum_fusion.3), channel_id=1, source_target_pairs={{0,12},{4,8},{8,4},{12,0},{16,28},{20,24},{24,20},{28,16},{1,13},{... | collective-permute-start | bytes 589832 | tf_op jit(solution)/shard_map/ppermute | solution.py:301
  70.3 10.9 %collective-permute-start.19 = (bf16[64,1536]{1,0:T(8,128)(2,1)S(1)}, bf16[64,1536]{1,0:T(8,128)(2,1)S(1)}, u32[]{:S(2)}, u32[]{:S(2)}) collective-permute-start(bf16[64,1536]{1,0:T(8,128)(2,1)S(1)} %pad_maximum_fusion.1), channel_id=1, source_target_pairs={{0,8},{4,12},{8,0},{12,4},{16,24},{20,28},{24,16},{28,20},{1,9},{5... | collective-permute-start | bytes 589832 | tf_op jit(solution)/shard_map/ppermute | solution.py:301
  71.9 9.3 %collective-permute-start.20 = (bf16[64,1536]{1,0:T(8,128)(2,1)S(1)}, bf16[64,1536]{1,0:T(8,128)(2,1)S(1)}, u32[]{:S(2)}, u32[]{:S(2)}) collective-permute-start(bf16[64,1536]{1,0:T(8,128)(2,1)S(1)} %pad_maximum_fusion.2), channel_id=1, source_target_pairs={{0,4},{4,0},{8,12},{12,8},{16,20},{20,16},{24,28},{28,24},{1,5},{5... | collective-permute-start | bytes 589832 | tf_op jit(solution)/shard_map/ppermute | solution.py:301
  81.4 7.5 %collective-permute-start.21 = (bf16[32,1536]{1,0:T(8,128)(2,1)S(1)}, bf16[32,1536]{1,0:T(8,128)(2,1)S(1)}, u32[]{:S(2)}, u32[]{:S(2)}) collective-permute-start(bf16[32,1536]{1,0:T(8,128)(2,1)S(1)} %get-tuple-element.108), channel_id=1, source_target_pairs={{0,8},{4,12},{8,0},{12,4},{16,24},{20,28},{24,16},{28,20},{1,9},{5... | collective-permute-start | bytes 294920 | tf_op jit(solution)/shard_map/ppermute | solution.py:301
  81.9 7.0 %collective-permute-start.22 = (bf16[32,1536]{1,0:T(8,128)(2,1)S(1)}, bf16[32,1536]{1,0:T(8,128)(2,1)S(1)}, u32[]{:S(2)}, u32[]{:S(2)}) collective-permute-start(bf16[32,1536]{1,0:T(8,128)(2,1)S(1)} %get-tuple-element.109), channel_id=1, source_target_pairs={{0,4},{4,0},{8,12},{12,8},{16,20},{20,16},{24,28},{28,24},{1,5},{5... | collective-permute-start | bytes 294920 | tf_op jit(solution)/shard_map/ppermute | solution.py:301
  83.3 5.8 %collective-permute-start.23 = (bf16[32,1536]{1,0:T(8,128)(2,1)S(1)}, bf16[32,1536]{1,0:T(8,128)(2,1)S(1)}, u32[]{:S(2)}, u32[]{:S(2)}) collective-permute-start(bf16[32,1536]{1,0:T(8,128)(2,1)S(1)} %get-tuple-element.110), channel_id=1, source_target_pairs={{0,12},{4,8},{8,4},{12,0},{16,28},{20,24},{24,20},{28,16},{1,13},{... | collective-permute-start | bytes 294920 | tf_op jit(solution)/shard_map/ppermute | solution.py:301
  84.9 4.6 %collective-permute-start.24 = (bf16[32,1536]{1,0:T(8,128)(2,1)S(1)}, bf16[32,1536]{1,0:T(8,128)(2,1)S(1)}, u32[]{:S(2)}, u32[]{:S(2)}) collective-permute-start(bf16[32,1536]{1,0:T(8,128)(2,1)S(1)} %add_convert_fusion.11), channel_id=1, source_target_pairs={{0,2},{1,3},{2,0},{3,1},{4,6},{5,7},{6,4},{7,5},{8,10},{9,11},{10,... | collective-permute-start | bytes 294920 | tf_op jit(solution)/shard_map/ppermute | solution.py:301
  89.7 10.7 %collective-permute-start.25 = (bf16[32,3072]{1,0:T(8,128)(2,1)S(1)}, bf16[32,3072]{1,0:T(8,128)(2,1)S(1)}, u32[]{:S(2)}, u32[]{:S(2)}) collective-permute-start(bf16[32,3072]{1,0:T(8,128)(2,1)S(1)} %pad_maximum_fusion.4), channel_id=1, source_target_pairs={{0,16},{4,20},{8,24},{12,28},{16,0},{20,4},{24,8},{28,12},{1,17},{... | collective-permute-start | bytes 589832 | tf_op jit(solution)/shard_map/ppermute | solution.py:301
  100.5 9.1 %collective-permute-start.28 = (bf16[32,3072]{1,0:T(8,128)(2,1)S(1)}, bf16[32,3072]{1,0:T(8,128)(2,1)S(1)}, u32[]{:S(2)}, u32[]{:S(2)}) collective-permute-start(bf16[32,3072]{1,0:T(8,128)(2,1)S(1)} %add_convert_fusion.2), channel_id=1, source_target_pairs={{0,12},{4,8},{8,4},{12,0},{16,28},{20,24},{24,20},{28,16},{1,13},{... | collective-permute-start | bytes 589832 | tf_op jit(solution)/shard_map/ppermute | solution.py:301
  100.8 10.8 %collective-permute-start.27 = (bf16[32,3072]{1,0:T(8,128)(2,1)S(1)}, bf16[32,3072]{1,0:T(8,128)(2,1)S(1)}, u32[]{:S(2)}, u32[]{:S(2)}) collective-permute-start(bf16[32,3072]{1,0:T(8,128)(2,1)S(1)} %add_convert_fusion.2), channel_id=1, source_target_pairs={{0,4},{4,0},{8,12},{12,8},{16,20},{20,16},{24,28},{28,24},{1,5},{5... | collective-permute-start | bytes 589832 | tf_op jit(solution)/shard_map/ppermute | solution.py:301
  101.8 9.8 %collective-permute-start.26 = (bf16[32,3072]{1,0:T(8,128)(2,1)S(1)}, bf16[32,3072]{1,0:T(8,128)(2,1)S(1)}, u32[]{:S(2)}, u32[]{:S(2)}) collective-permute-start(bf16[32,3072]{1,0:T(8,128)(2,1)S(1)} %add_convert_fusion.2), channel_id=1, source_target_pairs={{0,8},{4,12},{8,0},{12,4},{16,24},{20,28},{24,16},{28,20},{1,9},{5... | collective-permute-start | bytes 589832 | tf_op jit(solution)/shard_map/ppermute | solution.py:301

commit v3 on v1

--- a/solution.py
+++ b/solution.py
@@ -10,6 +10,7 @@
 EXPERTS = 8
 MOST = 80
 UNIT_TILE = 512
+HIDDEN_TILE = 1024
 FEATURE_TILE = 512
 BF16 = jnp.bfloat16
 F32 = jnp.float32
@@ -183,7 +184,7 @@
 def hidden_grads(pieces, slot, weight, act, slope, w_down):
     experts, blocks, tokens = slot.shape
     _, features, units = w_down.shape
-    tile = min(UNIT_TILE, units)
+    tile = min(HIDDEN_TILE, units)
     tiles = units // tile
     slots = blocks * MOST
     unit = pl.BlockSpec((1, slots, tile), lambda i: (i // tiles, 0, i % tiles))

time: 113 us -> 112 us (level)
  no operation moved by 1% of the time
where the time goes in v3:
time: 112 us
  Pallas kernels  63.2 us (56%)
  starting transfers between devices  27.9 us (25%)
  waiting for transfers between devices  14.5 us (13%)
  other arithmetic  3.85 us (3%)
  local copies, waits for them, and re-layouts  1.54 us (1%)
    ppermute x29, starting transfers between devices, flip(): return lax.ppermute(value, axis, [(i, i ^ bit) for i in range(count)])  27.9 us
    pallas_call x4, Pallas kernels, weight_grads(): pl.pallas_call(weights_kernel, grid=(steps,), in_specs=[pl.BlockSpec((1,...  22 us
    pallas_call x2, Pallas kernels, input_sums(): pl.pallas_call(functools.partial(inputs_kernel, groups), grid=(steps,), i...  16.2 us
    pallas_call x1, Pallas kernels, forward(): pl.pallas_call(functools.partial(forward_kernel, len(pieces)), grid=(expe...  15.9 us
    ppermute x29, waiting for transfers between devices, flip(): return lax.ppermute(value, axis, [(i, i ^ bit) for i in range(count)])  14.5 us
    pallas_call x1, Pallas kernels, hidden_grads(): pl.pallas_call(functools.partial(hidden_kernel, len(pieces)), grid=(exper...  9.17 us
  transfers between devices with their start and end apart: 29, of which 11 were waited for; matrix products, arithmetic and copies ran while one was open for 3% of the time, Pallas kernels for 41%

profile of v3, /device:TPU:0, one launch (start us, length us, event | category | flops | bytes accessed | tf_op | source)
XLA Modules:
  0.0 112.1 jit_solution(15903800703141278309)
XLA Ops:
  0.7 1.1 constant_dynamic-slice_fusion
  1.7 0.5 collective-permute-start
  2.3 2.6 %collective-permute-start.5 = (bf16[32,3072]{1,0:T(8,128)(2,1)S(1)}, bf16[32,3072]{1,0:T(8,128)(2,1)S(1)}, u32[]{:S(2)}, u32[]{:S(2)}) collective-permute-start(bf16[32,3072]{1,0:T(8,128)(2,1)S(1)} %get-tuple-element.71), channel_id=1, source_target_pairs={{0,2},{1,3},{2,0},{3,1},{4,6},{5,7},{6,4},{7,5},{8,10},{9,11},{10,... | collective-permute-start | bytes 589832 | tf_op jit(solution)/shard_map/ppermute | solution.py:302
  4.9 5.7 %collective-permute-done.5.refs_2_ = bf16[32,3072]{1,0:T(8,128)(2,1)S(1)} collective-permute-done((bf16[32,3072]{1,0:T(8,128)(2,1)S(1)}, bf16[32,3072]{1,0:T(8,128)(2,1)S(1)}, u32[]{:S(2)}, u32[]{:S(2)}) %collective-permute-start.5) | collective-permute-done | bytes 196640 | tf_op jit(solution)/shard_map/ppermute | solution.py:302
  10.6 2.0 %collective-permute-start.8 = (bf16[32,3072]{1,0:T(8,128)(2,1)S(1)}, bf16[32,3072]{1,0:T(8,128)(2,1)S(1)}, u32[]{:S(2)}, u32[]{:S(2)}) collective-permute-start(bf16[32,3072]{1,0:T(8,128)(2,1)S(1)} %collective-permute-done.5.refs_2_), channel_id=1, source_target_pairs={{0,8},{4,12},{8,0},{12,4},{16,24},{20,28},{24,16},{28,20},{1,9},{5... | collective-permute-start | bytes 589832 | tf_op jit(solution)/shard_map/ppermute | solution.py:302
  12.6 1.5 %collective-permute-start.7 = (bf16[32,3072]{1,0:T(8,128)(2,1)S(1)}, bf16[32,3072]{1,0:T(8,128)(2,1)S(1)}, u32[]{:S(2)}, u32[]{:S(2)}) collective-permute-start(bf16[32,3072]{1,0:T(8,128)(2,1)S(1)} %collective-permute-done.5.refs_2_), channel_id=1, source_target_pairs={{0,4},{4,0},{8,12},{12,8},{16,20},{20,16},{24,28},{28,24},{1,5},{5... | collective-permute-start | bytes 589832 | tf_op jit(solution)/shard_map/ppermute | solution.py:302
  14.1 0.7 fusion.1
  14.9 0.7 select_reduce_fusion
  15.7 1.6 %collective-permute-start.2 = (f32[2,2,128]{2,0,1:T(2,128)S(1)}, f32[2,2,128]{2,0,1:T(2,128)S(1)}, u32[]{:S(2)}, u32[]{:S(2)}) collective-permute-start(f32[2,2,128]{2,0,1:T(2,128)S(1)} %get-tuple-element.148), channel_id=1, source_target_pairs={{0,2},{1,3},{2,0},{3,1},{4,6},{5,7},{6,4},{7,5},{8,10},{9,11},{10,... | collective-permute-start | bytes 6152 | tf_op jit(solution)/shard_map/ppermute | solution.py:302
  17.3 0.3 collective-permute-start.3
  17.6 1.5 %collective-permute-start.13 = (bf16[128,3072]{1,0:T(8,128)(2,1)}, bf16[128,3072]{1,0:T(8,128)(2,1)S(1)}, u32[]{:S(2)}, u32[]{:S(2)}) collective-permute-start(bf16[128,3072]{1,0:T(8,128)(2,1)} %refs_0_.1), channel_id=1, source_target_pairs={{0,2},{1,3},{2,0},{3,1},{4,6},{5,7},{6,4},{7,5},{8,10},{9,11},{10,... | collective-permute-start | bytes 2359304 | tf_op jit(solution)/shard_map/ppermute | solution.py:302
  19.2 0.4 collective-permute-start.10
  19.7 0.6 collective-permute-done.3
  21.1 0.2 iota_compare_fusion
  21.3 0.2 add_convert_fusion.1.back
  21.5 0.4 collective-permute-start.4
  22.0 15.9 %shard_map.94 = (bf16[2,320,3072]{2,1,0:T(8,128)(2,1)}, f32[2,320,1024]{2,1,0:T(8,128)}, f32[2,320,1024]{2,1,0:T(8,128)}) custom-call(bf16[128,3072]{1,0:T(8,128)(2,1)} %refs_0_, bf16[128,3072]{1,0:T(8,128)(2,1)} %copy-done.2, bf16[32,3072]{1,0:T(8,128)(2,1)S(1)} %collective-permute-done.5.refs_2_, bf16[32,3072]{1,0:T(8,128)(2,1)S(1)} %collective-permute-done.6.refs_3_, ...), custom_call_target="tpu_custom_call" | custom-call | flops 8053063680 | bytes 25165824 | tf_op jit(solution)/shard_map/pallas_call | solution.py:144
  37.9 0.2 collective-permute-start.14
  38.1 2.1 %collective-permute-done.14.refs_3_ = bf16[128,3072]{1,0:T(8,128)(2,1)S(1)} collective-permute-done((bf16[128,3072]{1,0:T(8,128)(2,1)S(1)}, bf16[128,3072]{1,0:T(8,128)(2,1)S(1)}, u32[]{:S(2)}, u32[]{:S(2)}) %collective-permute-start.14) | collective-permute-done | bytes 786464 | tf_op jit(solution)/shard_map/ppermute | solution.py:302
  40.3 9.2 %shard_map.95 = (bf16[2,320,1024]{2,1,0:T(8,128)(2,1)S(1)}, bf16[2,320,1024]{2,1,0:T(8,128)(2,1)S(1)}) custom-call(bf16[128,3072]{1,0:T(8,128)(2,1)S(1)} %copy-done.1, bf16[128,3072]{1,0:T(8,128)(2,1)S(1)} %collective-permute-done.4.refs_1_, bf16[128,3072]{1,0:T(8,128)(2,1)S(1)} %collective-permute-done.13.refs_2_, ...), custom_call_target="tpu_custom_call" | custom-call | flops 4026531840 | bytes 12582912 | tf_op jit(solution)/shard_map/pallas_call | solution.py:191
  49.4 8.1 %shard_map.97 = (bf16[256,1536]{1,0:T(8,128)(2,1)S(1)}, bf16[256,1536]{1,0:T(8,128)(2,1)S(1)}) custom-call(bf16[4,128,160]{2,1,0:T(8,128)(2,1)S(1)} %add_convert_fusion.1.back, bf16[2,320,1024]{2,1,0:T(8,128)(2,1)S(1)} %get-tuple-element.78.gate_grad, bf16[2,320,1024]{2,1,0:T(8,128)(2,1)S(1)} %get-tuple-element.79.up_grad, bf16[2,3072,1024]{2,1,0:T(8,128)(2,1)} %w_gate.3, ...), custom_call_target="tpu_custom_call" | custom-call | flops 4026531840 | bytes 12582912 | tf_op jit(solution)/shard_map/pallas_call | solution.py:228
  57.6 0.2 collective-permute-start.16
  57.8 8.1 %shard_map.96 = (bf16[256,1536]{1,0:T(8,128)(2,1)S(1)}, bf16[256,1536]{1,0:T(8,128)(2,1)S(1)}) custom-call(bf16[4,128,160]{2,1,0:T(8,128)(2,1)S(1)} %add_convert_fusion.1.back, bf16[2,320,1024]{2,1,0:T(8,128)(2,1)S(1)} %get-tuple-element.78.gate_grad, bf16[2,320,1024]{2,1,0:T(8,128)(2,1)S(1)} %get-tuple-element.79.up_grad, bf16[2,3072,1024]{2,1,0:T(8,128)(2,1)} %w_gate.3, ...), custom_call_target="tpu_custom_call" | custom-call | flops 4026531840 | bytes 12582912 | tf_op jit(solution)/shard_map/pallas_call | solution.py:228
  65.9 0.4 collective-permute-start.15
  66.5 1.2 %collective-permute-start.17 = (bf16[128,1536]{1,0:T(8,128)(2,1)S(1)}, bf16[128,1536]{1,0:T(8,128)(2,1)S(1)}, u32[]{:S(2)}, u32[]{:S(2)}) collective-permute-start(bf16[128,1536]{1,0:T(8,128)(2,1)S(1)} %slice.175), channel_id=1, source_target_pairs={{0,2},{1,3},{2,0},{3,1},{4,6},{5,7},{6,4},{7,5},{8,10},{9,11},{10,... | collective-permute-start | bytes 1179656 | tf_op jit(solution)/shard_map/ppermute | solution.py:302
  67.8 0.5 collective-permute-done.15
  68.5 1.7 %collective-permute-start.18 = (bf16[64,1536]{1,0:T(8,128)(2,1)S(1)}, bf16[64,1536]{1,0:T(8,128)(2,1)S(1)}, u32[]{:S(2)}, u32[]{:S(2)}) collective-permute-start(bf16[64,1536]{1,0:T(8,128)(2,1)S(1)} %pad_maximum_fusion.3), channel_id=1, source_target_pairs={{0,12},{4,8},{8,4},{12,0},{16,28},{20,24},{24,20},{28,16},{1,13},{... | collective-permute-start | bytes 589832 | tf_op jit(solution)/shard_map/ppermute | solution.py:302
  70.1 0.4 collective-permute-start.19
  70.6 1.4 %collective-permute-start.20 = (bf16[64,1536]{1,0:T(8,128)(2,1)S(1)}, bf16[64,1536]{1,0:T(8,128)(2,1)S(1)}, u32[]{:S(2)}, u32[]{:S(2)}) collective-permute-start(bf16[64,1536]{1,0:T(8,128)(2,1)S(1)} %pad_maximum_fusion.2), channel_id=1, source_target_pairs={{0,4},{4,0},{8,12},{12,8},{16,20},{20,16},{24,28},{28,24},{1,5},{5... | collective-permute-start | bytes 589832 | tf_op jit(solution)/shard_map/ppermute | solution.py:302
  72.0 6.8 %shard_map.98 = (f32[2,3072,1024]{2,1,0:T(8,128)}, f32[2,3072,1024]{2,1,0:T(8,128)}) custom-call(bf16[2,320,3072]{2,1,0:T(8,128)(2,1)S(1)} %copy-done, bf16[2,320,1024]{2,1,0:T(8,128)(2,1)S(1)} %get-tuple-element.78.gate_grad, bf16[2,320,1024]{2,1,0:T(8,128)(2,1)S(1)} %get-tuple-element.79.up_grad), custom_call_target="tpu_custom_call" | custom-call | flops 2684354560 | bytes 16777216 | tf_op jit(solution)/shard_map/pallas_call | solution.py:267
  78.9 1.0 collective-permute-done.19
  79.9 0.9 collective-permute-done.20
  81.0 0.6 collective-permute-start.21
  81.6 1.4 %collective-permute-start.22 = (bf16[32,1536]{1,0:T(8,128)(2,1)S(1)}, bf16[32,1536]{1,0:T(8,128)(2,1)S(1)}, u32[]{:S(2)}, u32[]{:S(2)}) collective-permute-start(bf16[32,1536]{1,0:T(8,128)(2,1)S(1)} %get-tuple-element.97), channel_id=1, source_target_pairs={{0,4},{4,0},{8,12},{12,8},{16,20},{20,16},{24,28},{28,24},{1,5},{5... | collective-permute-start | bytes 294920 | tf_op jit(solution)/shard_map/ppermute | solution.py:302
  83.0 1.5 %collective-permute-start.23 = (bf16[32,1536]{1,0:T(8,128)(2,1)S(1)}, bf16[32,1536]{1,0:T(8,128)(2,1)S(1)}, u32[]{:S(2)}, u32[]{:S(2)}) collective-permute-start(bf16[32,1536]{1,0:T(8,128)(2,1)S(1)} %get-tuple-element.98), channel_id=1, source_target_pairs={{0,12},{4,8},{8,4},{12,0},{16,28},{20,24},{24,20},{28,16},{1,13},{... | collective-permute-start | bytes 294920 | tf_op jit(solution)/shard_map/ppermute | solution.py:302
  84.5 1.1 %collective-permute-start.24 = (bf16[32,1536]{1,0:T(8,128)(2,1)S(1)}, bf16[32,1536]{1,0:T(8,128)(2,1)S(1)}, u32[]{:S(2)}, u32[]{:S(2)}) collective-permute-start(bf16[32,1536]{1,0:T(8,128)(2,1)S(1)} %add_convert_fusion.11), channel_id=1, source_target_pairs={{0,2},{1,3},{2,0},{3,1},{4,6},{5,7},{6,4},{7,5},{8,10},{9,11},{10,... | collective-permute-start | bytes 294920 | tf_op jit(solution)/shard_map/ppermute | solution.py:302
  85.7 2.8 %shard_map.99 = (f32[2,3072,1024]{2,1,0:T(8,128)}, f32[2,3072,1024]{2,1,0:T(8,128)}) custom-call(bf16[2,320,3072]{2,1,0:T(8,128)(2,1)S(1)} %copy-done, bf16[2,320,1024]{2,1,0:T(8,128)(2,1)S(1)} %get-tuple-element.78.gate_grad, bf16[2,320,1024]{2,1,0:T(8,128)(2,1)S(1)} %get-tuple-element.79.up_grad, ...), custom_call_target="tpu_custom_call", output_to_operand_aliasing={{0}: (3, {}), {1}: (4, {})} | custom-call | flops 671088640 | bytes 4194304 | tf_op jit(solution)/shard_map/pallas_call | solution.py:267
  88.5 0.6 collective-permute-done.24
  89.3 2.6 %collective-permute-start.25 = (bf16[32,3072]{1,0:T(8,128)(2,1)S(1)}, bf16[32,3072]{1,0:T(8,128)(2,1)S(1)}, u32[]{:S(2)}, u32[]{:S(2)}) collective-permute-start(bf16[32,3072]{1,0:T(8,128)(2,1)S(1)} %pad_maximum_fusion.4), channel_id=1, source_target_pairs={{0,16},{4,20},{8,24},{12,28},{16,0},{20,4},{24,8},{28,12},{1,17},{... | collective-permute-start | bytes 589832 | tf_op jit(solution)/shard_map/ppermute | solution.py:302
  92.0 6.8 %shard_map.100 = (f32[2,3072,1024]{2,1,0:T(8,128)}, f32[2,3072,1024]{2,1,0:T(8,128)}) custom-call(bf16[2,320,3072]{2,1,0:T(8,128)(2,1)S(1)} %copy-done, bf16[2,320,1024]{2,1,0:T(8,128)(2,1)S(1)} %get-tuple-element.78.gate_grad, bf16[2,320,1024]{2,1,0:T(8,128)(2,1)S(1)} %get-tuple-element.79.up_grad, ...), custom_call_target="tpu_custom_call", output_to_operand_aliasing={{0}: (3, {}), {1}: (4, {})} | custom-call | flops 2684354560 | bytes 16777216 | tf_op jit(solution)/shard_map/pallas_call | solution.py:267
  98.8 0.7 collective-permute-done.25
  99.6 0.8 collective-permute-start.28
  100.3 0.9 collective-permute-start.27
  101.3 1.8 %collective-permute-start.26 = (bf16[32,3072]{1,0:T(8,128)(2,1)S(1)}, bf16[32,3072]{1,0:T(8,128)(2,1)S(1)}, u32[]{:S(2)}, u32[]{:S(2)}) collective-permute-start(bf16[32,3072]{1,0:T(8,128)(2,1)S(1)} %add_convert_fusion.2), channel_id=1, source_target_pairs={{0,8},{4,12},{8,0},{12,4},{16,24},{20,28},{24,16},{28,20},{1,9},{5... | collective-permute-start | bytes 589832 | tf_op jit(solution)/shard_map/ppermute | solution.py:302
  103.1 5.5 %shard_map.101 = (f32[2,3072,1024]{2,1,0:T(8,128)}, f32[2,3072,1024]{2,1,0:T(8,128)}) custom-call(bf16[2,320,3072]{2,1,0:T(8,128)(2,1)S(1)} %copy-done, bf16[2,320,1024]{2,1,0:T(8,128)(2,1)S(1)} %get-tuple-element.78.gate_grad, bf16[2,320,1024]{2,1,0:T(8,128)(2,1)S(1)} %get-tuple-element.79.up_grad, ...), custom_call_target="tpu_custom_call", output_to_operand_aliasing={{0}: (3, {}), {1}: (4, {})} | custom-call | flops 2013265920 | bytes 12582912 | tf_op jit(solution)/shard_map/pallas_call | solution.py:267
  108.6 1.9 %collective-permute-done.27 = bf16[32,3072]{1,0:T(8,128)(2,1)S(1)} collective-permute-done((bf16[32,3072]{1,0:T(8,128)(2,1)S(1)}, bf16[32,3072]{1,0:T(8,128)(2,1)S(1)}, u32[]{:S(2)}, u32[]{:S(2)}) %collective-permute-start.27) | collective-permute-done | bytes 196640 | tf_op jit(solution)/shard_map/ppermute | solution.py:302
  110.5 0.4 collective-permute-done.26
  111.1 1.0 reverse_select_fusion
  (63 shorter events, 2.2 us)
Async XLA Ops:
  1.7 12.4 %collective-permute-start = (bf16[128,3072]{1,0:T(8,128)(2,1)}, bf16[128,3072]{1,0:T(8,128)(2,1)S(1)}, u32[]{:S(2)}, u32[]{:S(2)}) collective-permute-start(bf16[128,3072]{1,0:T(8,128)(2,1)} %refs_0_), channel_id=1, source_target_pairs={{0,1},{1,0},{2,3},{3,2},{4,5},{5,4},{6,7},{7,6},{8,9},{9,8},{10,11... | collective-permute-start | bytes 2359304 | tf_op jit(solution)/shard_map/ppermute | solution.py:302
  2.3 8.4 %collective-permute-start.5 = (bf16[32,3072]{1,0:T(8,128)(2,1)S(1)}, bf16[32,3072]{1,0:T(8,128)(2,1)S(1)}, u32[]{:S(2)}, u32[]{:S(2)}) collective-permute-start(bf16[32,3072]{1,0:T(8,128)(2,1)S(1)} %get-tuple-element.71), channel_id=1, source_target_pairs={{0,2},{1,3},{2,0},{3,1},{4,6},{5,7},{6,4},{7,5},{8,10},{9,11},{10,... | collective-permute-start | bytes 589832 | tf_op jit(solution)/shard_map/ppermute | solution.py:302
  4.8 12.5 %collective-permute-start.6 = (bf16[32,3072]{1,0:T(8,128)(2,1)S(1)}, bf16[32,3072]{1,0:T(8,128)(2,1)S(1)}, u32[]{:S(2)}, u32[]{:S(2)}) collective-permute-start(bf16[32,3072]{1,0:T(8,128)(2,1)S(1)} %get-tuple-element.72), channel_id=1, source_target_pairs={{0,2},{1,3},{2,0},{3,1},{4,6},{5,7},{6,4},{7,5},{8,10},{9,11},{10,... | collective-permute-start | bytes 589832 | tf_op jit(solution)/shard_map/ppermute | solution.py:302
  10.6 7.0 %collective-permute-start.8 = (bf16[32,3072]{1,0:T(8,128)(2,1)S(1)}, bf16[32,3072]{1,0:T(8,128)(2,1)S(1)}, u32[]{:S(2)}, u32[]{:S(2)}) collective-permute-start(bf16[32,3072]{1,0:T(8,128)(2,1)S(1)} %collective-permute-done.5.refs_2_), channel_id=1, source_target_pairs={{0,8},{4,12},{8,0},{12,4},{16,24},{20,28},{24,16},{28,20},{1,9},{5... | collective-permute-start | bytes 589832 | tf_op jit(solution)/shard_map/ppermute | solution.py:302
  12.6 6.5 %collective-permute-start.7 = (bf16[32,3072]{1,0:T(8,128)(2,1)S(1)}, bf16[32,3072]{1,0:T(8,128)(2,1)S(1)}, u32[]{:S(2)}, u32[]{:S(2)}) collective-permute-start(bf16[32,3072]{1,0:T(8,128)(2,1)S(1)} %collective-permute-done.5.refs_2_), channel_id=1, source_target_pairs={{0,4},{4,0},{8,12},{12,8},{16,20},{20,16},{24,28},{28,24},{1,5},{5... | collective-permute-start | bytes 589832 | tf_op jit(solution)/shard_map/ppermute | solution.py:302
  14.1 7.9 %copy-start.2 = (bf16[128,3072]{1,0:T(8,128)(2,1)}, bf16[128,3072]{1,0:T(8,128)(2,1)S(1)}, u32[]{:S(2)}) copy-start(bf16[128,3072]{1,0:T(8,128)(2,1)S(1)} %collective-permute-done.refs_1_) | copy-start | bytes 2359300
  15.6 3.5 %collective-permute-start.1 = (f32[2,2,128]{2,0,1:T(2,128)S(1)}, f32[2,2,128]{2,0,1:T(2,128)S(1)}, u32[]{:S(2)}, u32[]{:S(2)}) collective-permute-start(f32[2,2,128]{2,0,1:T(2,128)S(1)} %get-tuple-element.147), channel_id=1, source_target_pairs={{0,1},{1,0},{2,3},{3,2},{4,5},{5,4},{6,7},{7,6},{8,9},{9,8},{10,11... | collective-permute-start | bytes 6152 | tf_op jit(solution)/shard_map/ppermute | solution.py:302
  15.7 3.9 %collective-permute-start.2 = (f32[2,2,128]{2,0,1:T(2,128)S(1)}, f32[2,2,128]{2,0,1:T(2,128)S(1)}, u32[]{:S(2)}, u32[]{:S(2)}) collective-permute-start(f32[2,2,128]{2,0,1:T(2,128)S(1)} %get-tuple-element.148), channel_id=1, source_target_pairs={{0,2},{1,3},{2,0},{3,1},{4,6},{5,7},{6,4},{7,5},{8,10},{9,11},{10,... | collective-permute-start | bytes 6152 | tf_op jit(solution)/shard_map/ppermute | solution.py:302
  17.3 3.0 %collective-permute-start.3 = (f32[2,2,128]{2,0,1:T(2,128)S(1)}, f32[2,2,128]{2,0,1:T(2,128)S(1)}, u32[]{:S(2)}, u32[]{:S(2)}) collective-permute-start(f32[2,2,128]{2,0,1:T(2,128)S(1)} %get-tuple-element.149), channel_id=1, source_target_pairs={{0,3},{1,2},{2,1},{3,0},{4,7},{5,6},{6,5},{7,4},{8,11},{9,10},{10,... | collective-permute-start | bytes 6152 | tf_op jit(solution)/shard_map/ppermute | solution.py:302
  17.6 20.3 %collective-permute-start.13 = (bf16[128,3072]{1,0:T(8,128)(2,1)}, bf16[128,3072]{1,0:T(8,128)(2,1)S(1)}, u32[]{:S(2)}, u32[]{:S(2)}) collective-permute-start(bf16[128,3072]{1,0:T(8,128)(2,1)} %refs_0_.1), channel_id=1, source_target_pairs={{0,2},{1,3},{2,0},{3,1},{4,6},{5,7},{6,4},{7,5},{8,10},{9,11},{10,... | collective-permute-start | bytes 2359304 | tf_op jit(solution)/shard_map/ppermute | solution.py:302
  19.1 2.4 %collective-permute-start.9 = (bf16[32,3072]{1,0:T(8,128)(2,1)S(1)}, bf16[32,3072]{1,0:T(8,128)(2,1)S(1)}, u32[]{:S(2)}, u32[]{:S(2)}) collective-permute-start(bf16[32,3072]{1,0:T(8,128)(2,1)S(1)} %collective-permute-done.5.refs_2_), channel_id=1, source_target_pairs={{0,1},{1,0},{2,3},{3,2},{4,5},{5,4},{6,7},{7,6},{8,9},{9,8},{10,11... | collective-permute-start | bytes 589832 | tf_op jit(solution)/shard_map/ppermute | solution.py:302
  19.2 2.8 %collective-permute-start.10 = (bf16[32,3072]{1,0:T(8,128)(2,1)S(1)}, bf16[32,3072]{1,0:T(8,128)(2,1)S(1)}, u32[]{:S(2)}, u32[]{:S(2)}) collective-permute-start(bf16[32,3072]{1,0:T(8,128)(2,1)S(1)} %collective-permute-done.6.refs_3_), channel_id=1, source_target_pairs={{0,1},{1,0},{2,3},{3,2},{4,5},{5,4},{6,7},{7,6},{8,9},{9,8},{10,11... | collective-permute-start | bytes 589832 | tf_op jit(solution)/shard_map/ppermute | solution.py:302
  19.6 2.3 %collective-permute-start.12 = (bf16[32,3072]{1,0:T(8,128)(2,1)S(1)}, bf16[32,3072]{1,0:T(8,128)(2,1)S(1)}, u32[]{:S(2)}, u32[]{:S(2)}) collective-permute-start(bf16[32,3072]{1,0:T(8,128)(2,1)S(1)} %collective-permute-done.8.refs_5_), channel_id=1, source_target_pairs={{0,1},{1,0},{2,3},{3,2},{4,5},{5,4},{6,7},{7,6},{8,9},{9,8},{10,11... | collective-permute-start | bytes 589832 | tf_op jit(solution)/shard_map/ppermute | solution.py:302
  20.3 1.6 %collective-permute-start.11 = (bf16[32,3072]{1,0:T(8,128)(2,1)S(1)}, bf16[32,3072]{1,0:T(8,128)(2,1)S(1)}, u32[]{:S(2)}, u32[]{:S(2)}) collective-permute-start(bf16[32,3072]{1,0:T(8,128)(2,1)S(1)} %collective-permute-done.7.refs_4_), channel_id=1, source_target_pairs={{0,1},{1,0},{2,3},{3,2},{4,5},{5,4},{6,7},{7,6},{8,9},{9,8},{10,11... | collective-permute-start | bytes 589832 | tf_op jit(solution)/shard_map/ppermute | solution.py:302
  21.5 18.7 %copy-start.1 = (bf16[128,3072]{1,0:T(8,128)(2,1)S(1)}, bf16[128,3072]{1,0:T(8,128)(2,1)}, u32[]{:S(2)}) copy-start(bf16[128,3072]{1,0:T(8,128)(2,1)} %refs_0_.1) | copy-start | bytes 2359300
  21.5 16.6 %collective-permute-start.4 = (bf16[128,3072]{1,0:T(8,128)(2,1)}, bf16[128,3072]{1,0:T(8,128)(2,1)S(1)}, u32[]{:S(2)}, u32[]{:S(2)}) collective-permute-start(bf16[128,3072]{1,0:T(8,128)(2,1)} %refs_0_.1), channel_id=1, source_target_pairs={{0,1},{1,0},{2,3},{3,2},{4,5},{5,4},{6,7},{7,6},{8,9},{9,8},{10,11... | collective-permute-start | bytes 2359304 | tf_op jit(solution)/shard_map/ppermute | solution.py:302
  37.9 2.4 %collective-permute-start.14 = (bf16[128,3072]{1,0:T(8,128)(2,1)S(1)}, bf16[128,3072]{1,0:T(8,128)(2,1)S(1)}, u32[]{:S(2)}, u32[]{:S(2)}) collective-permute-start(bf16[128,3072]{1,0:T(8,128)(2,1)S(1)} %collective-permute-done.13.refs_2_), channel_id=1, source_target_pairs={{0,1},{1,0},{2,3},{3,2},{4,5},{5,4},{6,7},{7,6},{8,9},{9,8},{10,11... | collective-permute-start | bytes 2359304 | tf_op jit(solution)/shard_map/ppermute | solution.py:302
  57.6 8.8 %collective-permute-start.16 = (bf16[256,1536]{1,0:T(8,128)(2,1)S(1)}, bf16[256,1536]{1,0:T(8,128)(2,1)S(1)}, u32[]{:S(2)}, u32[]{:S(2)}) collective-permute-start(bf16[256,1536]{1,0:T(8,128)(2,1)S(1)} %get-tuple-element.83), channel_id=1, source_target_pairs={{0,1},{1,0},{2,3},{3,2},{4,5},{5,4},{6,7},{7,6},{8,9},{9,8},{10,11... | collective-permute-start | bytes 2359304 | tf_op jit(solution)/shard_map/ppermute | solution.py:302
  65.9 2.4 %collective-permute-start.15 = (bf16[256,1536]{1,0:T(8,128)(2,1)S(1)}, bf16[256,1536]{1,0:T(8,128)(2,1)S(1)}, u32[]{:S(2)}, u32[]{:S(2)}) collective-permute-start(bf16[256,1536]{1,0:T(8,128)(2,1)S(1)} %get-tuple-element.81), channel_id=1, source_target_pairs={{0,1},{1,0},{2,3},{3,2},{4,5},{5,4},{6,7},{7,6},{8,9},{9,8},{10,11... | collective-permute-start | bytes 2359304 | tf_op jit(solution)/shard_map/ppermute | solution.py:302
  66.3 5.7 %copy-start = (bf16[2,320,3072]{2,1,0:T(8,128)(2,1)S(1)}, bf16[2,320,3072]{2,1,0:T(8,128)(2,1)}, u32[]{:S(2)}) copy-start(bf16[2,320,3072]{2,1,0:T(8,128)(2,1)} %get-tuple-element.117.rows) | copy-start | bytes 11796484
  66.5 14.3 %collective-permute-start.17 = (bf16[128,1536]{1,0:T(8,128)(2,1)S(1)}, bf16[128,1536]{1,0:T(8,128)(2,1)S(1)}, u32[]{:S(2)}, u32[]{:S(2)}) collective-permute-start(bf16[128,1536]{1,0:T(8,128)(2,1)S(1)} %slice.175), channel_id=1, source_target_pairs={{0,2},{1,3},{2,0},{3,1},{4,6},{5,7},{6,4},{7,5},{8,10},{9,11},{10,... | collective-permute-start | bytes 1179656 | tf_op jit(solution)/shard_map/ppermute | solution.py:302
  68.5 10.4 %collective-permute-start.18 = (bf16[64,1536]{1,0:T(8,128)(2,1)S(1)}, bf16[64,1536]{1,0:T(8,128)(2,1)S(1)}, u32[]{:S(2)}, u32[]{:S(2)}) collective-permute-start(bf16[64,1536]{1,0:T(8,128)(2,1)S(1)} %pad_maximum_fusion.3), channel_id=1, source_target_pairs={{0,12},{4,8},{8,4},{12,0},{16,28},{20,24},{24,20},{28,16},{1,13},{... | collective-permute-start | bytes 589832 | tf_op jit(solution)/shard_map/ppermute | solution.py:302
  70.1 9.8 %collective-permute-start.19 = (bf16[64,1536]{1,0:T(8,128)(2,1)S(1)}, bf16[64,1536]{1,0:T(8,128)(2,1)S(1)}, u32[]{:S(2)}, u32[]{:S(2)}) collective-permute-start(bf16[64,1536]{1,0:T(8,128)(2,1)S(1)} %pad_maximum_fusion.1), channel_id=1, source_target_pairs={{0,8},{4,12},{8,0},{12,4},{16,24},{20,28},{24,16},{28,20},{1,9},{5... | collective-permute-start | bytes 589832 | tf_op jit(solution)/shard_map/ppermute | solution.py:302
  70.6 10.2 %collective-permute-start.20 = (bf16[64,1536]{1,0:T(8,128)(2,1)S(1)}, bf16[64,1536]{1,0:T(8,128)(2,1)S(1)}, u32[]{:S(2)}, u32[]{:S(2)}) collective-permute-start(bf16[64,1536]{1,0:T(8,128)(2,1)S(1)} %pad_maximum_fusion.2), channel_id=1, source_target_pairs={{0,4},{4,0},{8,12},{12,8},{16,20},{20,16},{24,28},{28,24},{1,5},{5... | collective-permute-start | bytes 589832 | tf_op jit(solution)/shard_map/ppermute | solution.py:302
  81.0 7.5 %collective-permute-start.21 = (bf16[32,1536]{1,0:T(8,128)(2,1)S(1)}, bf16[32,1536]{1,0:T(8,128)(2,1)S(1)}, u32[]{:S(2)}, u32[]{:S(2)}) collective-permute-start(bf16[32,1536]{1,0:T(8,128)(2,1)S(1)} %get-tuple-element.96), channel_id=1, source_target_pairs={{0,8},{4,12},{8,0},{12,4},{16,24},{20,28},{24,16},{28,20},{1,9},{5... | collective-permute-start | bytes 294920 | tf_op jit(solution)/shard_map/ppermute | solution.py:302
  81.6 6.8 %collective-permute-start.22 = (bf16[32,1536]{1,0:T(8,128)(2,1)S(1)}, bf16[32,1536]{1,0:T(8,128)(2,1)S(1)}, u32[]{:S(2)}, u32[]{:S(2)}) collective-permute-start(bf16[32,1536]{1,0:T(8,128)(2,1)S(1)} %get-tuple-element.97), channel_id=1, source_target_pairs={{0,4},{4,0},{8,12},{12,8},{16,20},{20,16},{24,28},{28,24},{1,5},{5... | collective-permute-start | bytes 294920 | tf_op jit(solution)/shard_map/ppermute | solution.py:302
  83.0 5.5 %collective-permute-start.23 = (bf16[32,1536]{1,0:T(8,128)(2,1)S(1)}, bf16[32,1536]{1,0:T(8,128)(2,1)S(1)}, u32[]{:S(2)}, u32[]{:S(2)}) collective-permute-start(bf16[32,1536]{1,0:T(8,128)(2,1)S(1)} %get-tuple-element.98), channel_id=1, source_target_pairs={{0,12},{4,8},{8,4},{12,0},{16,28},{20,24},{24,20},{28,16},{1,13},{... | collective-permute-start | bytes 294920 | tf_op jit(solution)/shard_map/ppermute | solution.py:302
  84.5 4.6 %collective-permute-start.24 = (bf16[32,1536]{1,0:T(8,128)(2,1)S(1)}, bf16[32,1536]{1,0:T(8,128)(2,1)S(1)}, u32[]{:S(2)}, u32[]{:S(2)}) collective-permute-start(bf16[32,1536]{1,0:T(8,128)(2,1)S(1)} %add_convert_fusion.11), channel_id=1, source_target_pairs={{0,2},{1,3},{2,0},{3,1},{4,6},{5,7},{6,4},{7,5},{8,10},{9,11},{10,... | collective-permute-start | bytes 294920 | tf_op jit(solution)/shard_map/ppermute | solution.py:302
  89.3 10.2 %collective-permute-start.25 = (bf16[32,3072]{1,0:T(8,128)(2,1)S(1)}, bf16[32,3072]{1,0:T(8,128)(2,1)S(1)}, u32[]{:S(2)}, u32[]{:S(2)}) collective-permute-start(bf16[32,3072]{1,0:T(8,128)(2,1)S(1)} %pad_maximum_fusion.4), channel_id=1, source_target_pairs={{0,16},{4,20},{8,24},{12,28},{16,0},{20,4},{24,8},{28,12},{1,17},{... | collective-permute-start | bytes 589832 | tf_op jit(solution)/shard_map/ppermute | solution.py:302
  99.6 9.1 %collective-permute-start.28 = (bf16[32,3072]{1,0:T(8,128)(2,1)S(1)}, bf16[32,3072]{1,0:T(8,128)(2,1)S(1)}, u32[]{:S(2)}, u32[]{:S(2)}) collective-permute-start(bf16[32,3072]{1,0:T(8,128)(2,1)S(1)} %add_convert_fusion.2), channel_id=1, source_target_pairs={{0,12},{4,8},{8,4},{12,0},{16,28},{20,24},{24,20},{28,16},{1,13},{... | collective-permute-start | bytes 589832 | tf_op jit(solution)/shard_map/ppermute | solution.py:302
  100.3 10.2 %collective-permute-start.27 = (bf16[32,3072]{1,0:T(8,128)(2,1)S(1)}, bf16[32,3072]{1,0:T(8,128)(2,1)S(1)}, u32[]{:S(2)}, u32[]{:S(2)}) collective-permute-start(bf16[32,3072]{1,0:T(8,128)(2,1)S(1)} %add_convert_fusion.2), channel_id=1, source_target_pairs={{0,4},{4,0},{8,12},{12,8},{16,20},{20,16},{24,28},{28,24},{1,5},{5... | collective-permute-start | bytes 589832 | tf_op jit(solution)/shard_map/ppermute | solution.py:302
  101.3 9.6 %collective-permute-start.26 = (bf16[32,3072]{1,0:T(8,128)(2,1)S(1)}, bf16[32,3072]{1,0:T(8,128)(2,1)S(1)}, u32[]{:S(2)}, u32[]{:S(2)}) collective-permute-start(bf16[32,3072]{1,0:T(8,128)(2,1)S(1)} %add_convert_fusion.2), channel_id=1, source_target_pairs={{0,8},{4,12},{8,0},{12,4},{16,24},{20,28},{24,16},{28,20},{1,9},{5... | collective-permute-start | bytes 589832 | tf_op jit(solution)/shard_map/ppermute | solution.py:302
